TPU v7x, 256 devices: a whole 4x4x8 slice. The times are simulated.
256 devices in a mesh: cam: 8 (over x_lo, y), tm: 32 (over z, x_hi, core).
Axes of the slice: x: 4 (x_hi: 2, x_lo: 2; x = x_hi * 2 + x_lo), y: 4, z: 8, core: 2. Of those that a mesh axis runs over, the one named last changes fastest.
Arguments:
- latents: bfloat16 [8, 64, 16, 32, 256], P('cam', 'tm'), may hold values from -12 to 12
- cycle_position: int32 [8], replicated, may hold values from 0 to 7, as said below
- conv_first: bfloat16 [3, 3, 3, 256, 256], replicated, may hold values from -0.078125 to 0.078125
- conv_second: bfloat16 [3, 3, 3, 256, 256], replicated, may hold values from -0.078125 to 0.078125
- norm_gain: float32 [256], replicated, may hold values from 0.5 to 1.5
- norm_shift: float32 [256], replicated, may hold values from -3 to 3
- w_query: bfloat16 [256, 256], replicated, may hold values from -8 to 8
- w_key: bfloat16 [256, 256], replicated, may hold values from -8 to 8
- w_value: bfloat16 [256, 256], replicated, may hold values from -0.375 to 0.375
- w_out: bfloat16 [256, 256], replicated, may hold values from -0.375 to 0.375
- camera_table: float32 [8, 256], replicated, may hold values from -5 to 5
- side_embed: bfloat16 [2, 256], replicated, may hold values from -5 to 5
Outputs:
- block_out: bfloat16 [8, 64, 16, 32, 256], P('cam', 'tm')
Inputs may be any that keep to these rules, and one draw needn't show every extreme that they name: cycle_position[i] is the cycle place of the camera at index i of cam: the places 0 to 7 rotated, running forwards or backwards with the index, so cycle neighbours sit on neighbouring indices with wrap-around.
All inputs are finite; a program needn't handle non-finite values.
Results may differ from a plain program's by a relative error of at most 0.012.
The roundings to bfloat16 on the way count: a program that leaves them out, or rounds other values in their place, can miss the bound.
Values may be sent and summed in bfloat16 or wider, within the bound.
A program may use at most 64 MiB of HBM per device.

v0:
```python
import jax
import jax.numpy as jnp
from jax import lax
from jax.sharding import PartitionSpec as P

GROUPS = 32


def passed_along(block, axis, distance):
    devices = range(lax.axis_size(axis))
    route = [(i - distance, i) for i in devices if i - distance in devices]
    return lax.ppermute(block, axis, route)


def shifted(value, axis, by):
    length = lax.axis_size(axis)
    return lax.ppermute(value, axis, [(i, (i + by) % length) for i in range(length)])


def causal_conv(frames, past, kernel):
    count, rows, cols, chans = frames.shape
    full = jnp.concatenate([past, frames], axis=0)
    full = jnp.pad(full, ((0, 0), (1, 1), (1, 1), (0, 0)))
    total = jnp.zeros((count * rows * cols, kernel.shape[-1]), jnp.float32)
    for step_t in range(3):
        for step_r in range(3):
            for step_c in range(3):
                tap = full[
                    step_t : step_t + count, step_r : step_r + rows, step_c : step_c + cols
                ].reshape(-1, chans)
                total = total + jnp.dot(
                    tap, kernel[step_t, step_r, step_c], preferred_element_type=jnp.float32
                )
    return total.reshape(count, rows, cols, -1)


def attend_frame(query, keys, values, side_terms):
    half = keys.shape[0] // 2
    chans = query.shape[1]
    raw = jnp.einsum("qc,kc->qk", query, keys, preferred_element_type=jnp.float32)
    bias = jnp.concatenate(
        [
            jnp.broadcast_to(side_terms[:, 0:1], (query.shape[0], half)),
            jnp.broadcast_to(side_terms[:, 1:2], (query.shape[0], half)),
        ],
        axis=1,
    )
    scores = (raw + bias) * chans ** (-0.5)
    top = jnp.max(scores, axis=1, keepdims=True)
    expo = jnp.exp(scores - top)
    weight = (expo / jnp.sum(expo, axis=1, keepdims=True)).astype(jnp.bfloat16)
    return jnp.dot(weight, values, preferred_element_type=jnp.float32).astype(jnp.bfloat16)


def project_pair(frames, w_key, w_value):
    rows = frames.reshape(-1, frames.shape[-1])
    keys = jnp.dot(rows, w_key, preferred_element_type=jnp.float32).astype(jnp.bfloat16)
    values = jnp.dot(rows, w_value, preferred_element_type=jnp.float32).astype(jnp.bfloat16)
    return (keys, values)


def on_device(
    latents,
    cycle_position,
    conv_first,
    conv_second,
    norm_gain,
    norm_shift,
    w_query,
    w_key,
    w_value,
    w_out,
    camera_table,
    side_embed,
):
    frames = latents[0]
    count, rows_n, cols_n, chans = frames.shape
    at_start = lax.axis_index("tm") == 0
    past = passed_along(frames, "tm", 1)
    past = jnp.where(at_start, jnp.broadcast_to(frames[0:1], past.shape), past)
    first = causal_conv(frames, past, conv_first)
    grouped = first.reshape(count, rows_n, cols_n, GROUPS, chans // GROUPS)
    entries = count * lax.axis_size("tm") * rows_n * cols_n * (chans // GROUPS)
    total = lax.psum(jnp.sum(grouped, axis=(0, 1, 2, 4)), "tm")
    mean = total / entries
    dev = grouped - mean[:, None]
    spread = lax.psum(jnp.sum(dev * dev, axis=(0, 1, 2, 4)), "tm") / entries
    normed = (dev * lax.rsqrt(spread + 1e-05)[:, None]).reshape(
        count, rows_n, cols_n, chans
    ) * norm_gain + norm_shift
    hidden = jax.nn.silu(normed).astype(jnp.bfloat16)
    cameras = lax.axis_size("cam")
    me_index = lax.axis_index("cam")
    ids = jnp.arange(cameras, dtype=jnp.int32)
    my_place = jnp.sum(jnp.where(ids == me_index, cycle_position, 0))
    below_place = jnp.sum(jnp.where(ids == (me_index - 1) % cameras, cycle_position, 0))
    below_is_left = below_place == (my_place - 1) % cameras
    table_row = jnp.sum(jnp.where((ids == my_place)[:, None], camera_table, 0.0), axis=0)
    rows = hidden.reshape(-1, chans)
    extra = jnp.dot(table_row, w_query.astype(jnp.float32), precision=lax.Precision.HIGHEST)
    query = (jnp.dot(rows, w_query, preferred_element_type=jnp.float32) + extra).astype(
        jnp.bfloat16
    )
    hidden_below = shifted(hidden, "cam", 1)
    hidden_above = shifted(hidden, "cam", -1)
    keys_below, values_below = project_pair(hidden_below, w_key, w_value)
    keys_above, values_above = project_pair(hidden_above, w_key, w_value)
    keys_left = jnp.where(below_is_left, keys_below, keys_above)
    values_left = jnp.where(below_is_left, values_below, values_above)
    keys_right = jnp.where(below_is_left, keys_above, keys_below)
    values_right = jnp.where(below_is_left, values_above, values_below)
    cells = rows_n * cols_n
    side_terms = jnp.dot(query, side_embed.T, preferred_element_type=jnp.float32)
    keys = jnp.concatenate(
        [keys_left.reshape(count, cells, chans), keys_right.reshape(count, cells, chans)], axis=1
    )
    values = jnp.concatenate(
        [values_left.reshape(count, cells, chans), values_right.reshape(count, cells, chans)],
        axis=1,
    )
    attended = lax.map(
        lambda items: attend_frame(*items),
        (query.reshape(count, cells, chans), keys, values, side_terms.reshape(count, cells, 2)),
    )
    out_proj = jnp.dot(attended.reshape(-1, chans), w_out, preferred_element_type=jnp.float32)
    mixed = (
        (rows.astype(jnp.float32) + out_proj)
        .astype(jnp.bfloat16)
        .reshape(count, rows_n, cols_n, chans)
    )
    mixed_prev = passed_along(mixed, "tm", 1)
    mixed_prev = jnp.where(at_start, jnp.broadcast_to(mixed[0:1], mixed_prev.shape), mixed_prev)
    second = causal_conv(mixed, mixed_prev, conv_second)
    return (frames.astype(jnp.float32) + second).astype(jnp.bfloat16)[None]


def solution(mesh):
    in_specs = (
        P("cam", "tm", None, None, None),
        P(),
        P(),
        P(),
        P(),
        P(),
        P(),
        P(),
        P(),
        P(),
        P(),
        P(),
    )
    out_specs = P("cam", "tm", None, None, None)
    return jax.shard_map(
        on_device, mesh=mesh, in_specs=in_specs, out_specs=out_specs, check_vma=False
    )
```

profile of v0, /device:TPU:128, one launch (start us, length us, event | category | flops | bytes accessed | tf_op | source)
XLA Modules:
  0.0 217.3 jit_solution(14835019203041922780)
XLA Ops:
  0.0 2.0 collective-permute-start
  2.1 1.4 fusion.131
  4.0 0.6 iota_compare_fusion
  5.3 0.8 select_reduce_fusion
  6.1 1.0 fusion.135
  7.1 1.0 slice_bitcast_fusion
  8.2 6.3 %collective-permute-done = bf16[2,16,32,256]{3,2,1,0:T(8,128)(2,1)S(1)} collective-permute-done((bf16[2,16,32,256]{3,2,1,0:T(8,128)(2,1)}, bf16[2,16,32,256]{3,2,1,0:T(8,128)(2,1)S(1)}, u32[]{:S(2)}, u32[]{:S(2)}) %collective-permute-start) | collective-permute-done | bytes 524320 | tf_op jit(solution)/shard_map/ppermute | solution.py:12
  14.5 1.1 pad_maximum_fusion
  15.6 4.3 %pad_slice_fusion.24 = (bf16[2,16,32,256]{3,2,1,0:T(8,128)(2,1)S(1)}, bf16[2,16,32,256]{3,2,1,0:T(8,128)(2,1)S(1)}, bf16[2,16,32,256]{3,2,1,0:T(8,128)(2,1)S(1)}...) fusion(bf16[4,16,32,256]{3,2,1,0:T(8,128)(2,1)S(1)} %pad_maximu, ...), kind=kLoop, calls=%fused_computation.41 | loop fusion | bytes 11010048 | tf_op jit(solution)/shard_map/slice | solution.py:28
  20.0 0.8 pad_slice_fusion.25
  21.0 1.1 copy-done.3
  23.0 0.3 convolution_add_fusion.50
  23.3 0.3 convolution_add_fusion.49
  23.6 0.3 fusion.13
  25.1 0.3 convolution_add_fusion.43
  25.4 0.3 convolution_add_fusion.42
  25.7 0.3 convolution_add_fusion.41
  26.0 0.3 convolution_add_fusion.40
  26.3 0.3 convolution_add_fusion.39
  26.6 0.3 convolution_add_fusion.38
  26.9 0.3 convolution_add_fusion.37
  27.2 0.3 convolution_add_fusion.36
  27.5 0.3 convolution_add_fusion.35
  30.0 0.4 fusion.134
  30.6 65.0 %psum.14 = f32[32]{0:T(128)S(1)} all-reduce(f32[32]{0:T(128)S(1)} %reduce_sum.70), channel_id=1, replica_groups=mesh['cam'=8,'tm'=32] {'tm'}, use_global_device_ids=true, to_apply=%region_2.3 | all-reduce | flops 32 | bytes 256 | tf_op jit(solution)/shard_map/psum | solution.py:84
  96.2 65.0 %psum.15 = f32[32]{0:T(128)S(1)} all-reduce(f32[32]{0:T(128)S(1)} %reduce_sum.73), channel_id=1, replica_groups=mesh['cam'=8,'tm'=32] {'tm'}, use_global_device_ids=true, to_apply=%region_5.6 | all-reduce | flops 32 | bytes 256 | tf_op jit(solution)/shard_map/psum | solution.py:87
  161.4 0.3 multiply_convert_fusion
  161.7 4.0 %collective-permute-start.2 = (bf16[2,16,32,256]{3,2,1,0:T(8,128)(2,1)S(1)}, bf16[2,16,32,256]{3,2,1,0:T(8,128)(2,1)S(1)}, u32[]{:S(2)}, u32[]{:S(2)}) collective-permute-start(bf16[2,16,32,256]{3,2,1,0:T(8,128)(2,1)S(1)} %multiply_convert_fusion), channel_id=1, source_target_pairs={{0,224},{32,0},{64,32},{96,64},{128,96},{160,128},{192,160},{224,1... | collective-permute-start | bytes 1572872 | tf_op jit(solution)/shard_map/ppermute | solution.py:17
  165.8 0.3 multiply_convert_fusion.1
  166.7 10.3 %collective-permute-done.2 = bf16[2,16,32,256]{3,2,1,0:T(8,128)(2,1)S(1)} collective-permute-done((bf16[2,16,32,256]{3,2,1,0:T(8,128)(2,1)S(1)}, bf16[2,16,32,256]{3,2,1,0:T(8,128)(2,1)S(1)}, u32[]{:S(2)}, u32[]{:S(2)}) %collective-permute-start.2) | collective-permute-done | bytes 524320 | tf_op jit(solution)/shard_map/ppermute | solution.py:17
  177.6 3.7 %collective-permute-done.1 = bf16[2,16,32,256]{3,2,1,0:T(8,128)(2,1)S(1)} collective-permute-done((bf16[2,16,32,256]{3,2,1,0:T(8,128)(2,1)S(1)}, bf16[2,16,32,256]{3,2,1,0:T(8,128)(2,1)S(1)}, u32[]{:S(2)}, u32[]{:S(2)}) %collective-permute-start.1) | collective-permute-done | bytes 524320 | tf_op jit(solution)/shard_map/ppermute | solution.py:17
  181.9 1.1 pad_maximum_fusion.2
  183.0 4.2 %while.10 = (s32[]{:T(128)}, bf16[2,512,256]{2,1,0:T(8,128)(2,1)S(1)}, bf16[2,512,256]{2,1,0:T(8,128)(2,1)S(1)}, bf16[2,1024,256]{2,1,0:T(8,128)(2,1)S(1)}, f32[...) while((s32[]{:T(128)}, bf16[2,512,256]{2,1,0:T(8,128)(2,1)S(1)}, ...), condition=%wide.region_12.13_spmd, body=%wide.region_9.12_spmd.sunk | while | flops 541719552 | bytes 16285805 | solution.py:121
  183.3 0.6 fusion.214
  183.9 0.5 fusion.215
  184.5 0.5 fusion.216
  185.4 0.6 fusion.214
  186.0 0.5 fusion.215
  186.6 0.5 fusion.216
  187.2 0.3 fusion.15
  187.5 1.9 collective-permute-start.3
  189.5 12.2 %collective-permute-done.3 = bf16[2,16,32,256]{3,2,1,0:T(8,128)(2,1)S(1)} collective-permute-done((bf16[2,16,32,256]{3,2,1,0:T(8,128)(2,1)S(1)}, bf16[2,16,32,256]{3,2,1,0:T(8,128)(2,1)S(1)}, u32[]{:S(2)}, u32[]{:S(2)}) %collective-permute-start.3) | collective-permute-done | bytes 524320 | tf_op jit(solution)/shard_map/ppermute | solution.py:12
  201.8 4.3 %pad_slice_fusion = (bf16[2,16,32,256]{3,2,1,0:T(8,128)(2,1)S(1)}, bf16[2,16,32,256]{3,2,1,0:T(8,128)(2,1)S(1)}, bf16[2,16,32,256]{3,2,1,0:T(8,128)(2,1)S(1)}, b...) fusion(bf16[4,16,32,256]{3,2,1,0:T(8,128)(2,1)S(1)} %pad_maximu, ...), kind=kLoop, calls=%fused_computation.17 | loop fusion | bytes 11010048 | tf_op jit(solution)/shard_map/slice | solution.py:28
  206.2 0.8 pad_slice_fusion.1
  206.9 1.2 copy-done.4
  209.6 0.3 fusion.12
  212.7 0.3 convolution_add_fusion.11
  216.3 1.0 add_convert_fusion
  (96 shorter events, 15.5 us)
Async XLA Ops:
  0.0 177.0 %copy-start = (bf16[256,256]{1,0:T(8,128)(2,1)S(1)}, bf16[256,256]{1,0:T(8,128)(2,1)}, u32[]{:S(2)}) copy-start(bf16[256,256]{1,0:T(8,128)(2,1)} %param.22) | copy-start | bytes 393220
  0.0 14.4 %collective-permute-start = (bf16[2,16,32,256]{3,2,1,0:T(8,128)(2,1)}, bf16[2,16,32,256]{3,2,1,0:T(8,128)(2,1)S(1)}, u32[]{:S(2)}, u32[]{:S(2)}) collective-permute-start(bf16[2,16,32,256]{3,2,1,0:T(8,128)(2,1)} %bitcast.342), channel_id=1, source_target_pairs={{0,1},{1,2},{2,3},{3,4},{4,5},{5,6},{6,7},{7,8},{8,9},{9,10},{10,1... | collective-permute-start | bytes 1572872 | tf_op jit(solution)/shard_map/ppermute | solution.py:12
  19.9 1.0 copy-start.2
  20.0 2.2 copy-start.3
  29.6 131.7 %copy-start.9 = (f32[256]{0:T(256)S(1)}, f32[256]{0:T(256)}, u32[]{:S(2)}) copy-start(f32[256]{0:T(256)} %param.19) | copy-start | bytes 3076
  29.7 131.7 %copy-start.10 = (f32[256]{0:T(256)S(1)}, f32[256]{0:T(256)}, u32[]{:S(2)}) copy-start(f32[256]{0:T(256)} %param.18) | copy-start | bytes 3076
  30.0 136.1 %copy-start.7 = (bf16[256,256]{1,0:T(8,128)(2,1)S(1)}, bf16[256,256]{1,0:T(8,128)(2,1)}, u32[]{:S(2)}) copy-start(bf16[256,256]{1,0:T(8,128)(2,1)} %param.20) | copy-start | bytes 393220
  30.0 136.4 %copy-start.11 = (bf16[2,256]{1,0:T(2,128)(2,1)S(1)}, bf16[2,256]{1,0:T(2,128)(2,1)}, u32[]{:S(2)}) copy-start(bf16[2,256]{1,0:T(2,128)(2,1)} %param.25) | copy-start | bytes 3076
  95.8 81.5 %copy-start.6 = (bf16[256,256]{1,0:T(8,128)(2,1)S(1)}, bf16[256,256]{1,0:T(8,128)(2,1)}, u32[]{:S(2)}) copy-start(bf16[256,256]{1,0:T(8,128)(2,1)} %param.21) | copy-start | bytes 393220
  161.7 15.2 %collective-permute-start.2 = (bf16[2,16,32,256]{3,2,1,0:T(8,128)(2,1)S(1)}, bf16[2,16,32,256]{3,2,1,0:T(8,128)(2,1)S(1)}, u32[]{:S(2)}, u32[]{:S(2)}) collective-permute-start(bf16[2,16,32,256]{3,2,1,0:T(8,128)(2,1)S(1)} %multiply_convert_fusion), channel_id=1, source_target_pairs={{0,224},{32,0},{64,32},{96,64},{128,96},{160,128},{192,160},{224,1... | collective-permute-start | bytes 1572872 | tf_op jit(solution)/shard_map/ppermute | solution.py:17
  165.8 15.5 %collective-permute-start.1 = (bf16[2,16,32,256]{3,2,1,0:T(8,128)(2,1)S(1)}, bf16[2,16,32,256]{3,2,1,0:T(8,128)(2,1)S(1)}, u32[]{:S(2)}, u32[]{:S(2)}) collective-permute-start(bf16[2,16,32,256]{3,2,1,0:T(8,128)(2,1)S(1)} %multiply_convert_fusion), channel_id=1, source_target_pairs={{0,32},{32,64},{64,96},{96,128},{128,160},{160,192},{192,224},{224... | collective-permute-start | bytes 1572872 | tf_op jit(solution)/shard_map/ppermute | solution.py:17
  183.0 4.2 %copy-start.8 = (bf16[256,256]{1,0:T(8,128)(2,1)S(1)}, bf16[256,256]{1,0:T(8,128)(2,1)}, u32[]{:S(2)}) copy-start(bf16[256,256]{1,0:T(8,128)(2,1)} %param.23) | copy-start | bytes 393220
  183.3 1.2 copy-start.5
  185.4 1.2 copy-start.5
  187.5 14.1 %collective-permute-start.3 = (bf16[2,16,32,256]{3,2,1,0:T(8,128)(2,1)S(1)}, bf16[2,16,32,256]{3,2,1,0:T(8,128)(2,1)S(1)}, u32[]{:S(2)}, u32[]{:S(2)}) collective-permute-start(bf16[2,16,32,256]{3,2,1,0:T(8,128)(2,1)S(1)} %bitcast.346), channel_id=1, source_target_pairs={{0,1},{1,2},{2,3},{3,4},{4,5},{5,6},{6,7},{7,8},{8,9},{9,10},{10,1... | collective-permute-start | bytes 1572872 | tf_op jit(solution)/shard_map/ppermute | solution.py:12
  206.1 2.0 copy-start.4
  215.7 1.6 copy-start.1
where the time goes:
time: 218 us; the launch traced here: 217 us
  blocking collectives  130 us (60%)
  waiting for transfers between devices  32.5 us (15%)
  matrix products  21.3 us (10%)
  local copies, waits for them, and re-layouts  15.1 us (7%)
  other arithmetic  8.4 us (4%)
  starting transfers between devices  7.98 us (4%)
    psum x1, blocking collectives, on_device(): total = lax.psum(jnp.sum(grouped, axis=(0, 1, 2, 4)), 'tm')  65 us
    psum x1, blocking collectives, on_device(): spread = lax.psum(jnp.sum(dev * dev, axis=(0, 1, 2, 4)), 'tm') / entries  65 us
    ppermute x2, waiting for transfers between devices, passed_along(): return lax.ppermute(block, axis, route)  18.5 us
    dot_general x54, matrix products, causal_conv(): jnp.dot(tap, kernel[step_t, step_r, step_c], preferred_element_type=jnp.f...  16 us
    ppermute x2, waiting for transfers between devices, shifted(): lax.ppermute(value, axis, [(i, (i + by) % length) for i in range(length)])  14 us
    slice x4, local copies, waits for them, and re-layouts, causal_conv(): full[step_t:step_t + count, step_r:step_r + rows, step_c:step_c + cols]  10.1 us
  transfers between devices with their start and end apart: 4, of which 4 were waited for; matrix products, arithmetic and copies ran while one was open for 3% of the time, Pallas kernels for 0%

commit v1 on v0

v1 whole, which is shorter than its diff:
```python
import functools

import jax
import jax.numpy as jnp
from jax import lax
from jax.experimental import pallas as pl
from jax.experimental.pallas import tpu as pltpu
from jax.sharding import PartitionSpec as P

GROUPS = 32
F32 = jnp.float32
BF16 = jnp.bfloat16
MESH = pl.DeviceIdType.MESH
ROWS, COLS, CHANS = 16, 32, 256
CELLS = ROWS * COLS
TALL = CELLS + 2 * COLS


def dot(a, b):
    return jnp.dot(a, b, preferred_element_type=F32)


def dot_t(a, b):
    return lax.dot_general(a, b, (((1,), (1,)), ((), ())), preferred_element_type=F32)


def conv_terms(buf, w, terms):
    parts = []
    for ds in range(3):
        acc = jnp.zeros((CELLS, CHANS), F32)
        for slot, dt in terms:
            for dr in range(3):
                acc += dot(
                    buf[slot, pl.ds(dr * COLS, CELLS), :],
                    w[dt * 3 + dr, pl.ds(ds * CHANS, CHANS), :],
                )
        parts.append(acc)
    col = lax.rem(lax.broadcasted_iota(jnp.int32, (CELLS, CHANS), 0), COLS)
    left = jnp.where(col == 0, 0.0, pltpu.roll(parts[0], 1, 0))
    right = jnp.where(col == COLS - 1, 0.0, pltpu.roll(parts[2], CELLS - 1, 0))
    return parts[1] + left + right


def block_kernel(
    cams,
    tms,
    lat_ref,
    place_ref,
    w1_ref,
    w2_ref,
    gain_ref,
    shift_ref,
    wq_ref,
    wk_ref,
    wv_ref,
    wo_ref,
    table_ref,
    side_ref,
    out_ref,
    xb,
    mb,
    w1,
    w2,
    first,
    part,
    far,
    nbr,
    hid,
    query,
    st,
    fw,
    fw_in,
    place,
    gain,
    shift,
    wq,
    wk,
    wv,
    wo,
    table,
    side,
    lsem,
    hsend,
    hrecv,
    ssend,
    srecv,
    csend,
    crecv,
    fsend,
    frecv,
    msend,
    mrecv,
):
    cam = lax.axis_index("cam")
    tm = lax.axis_index("tm")
    cam_above = lax.rem(cam + 1, cams)
    cam_below = lax.rem(cam + cams - 1, cams)
    core = lax.rem(tm, 2)
    pair = tm + 1 - 2 * core
    after = (cam, lax.rem(tm + 1, tms))
    is_first = tm == 0
    is_last = tm == tms - 1

    def later(i):
        return (cam, lax.rem(tm + i, tms))

    def remote(src, dst, send, recv, to):
        return pltpu.make_async_remote_copy(
            src_ref=src,
            dst_ref=dst,
            send_sem=send,
            recv_sem=recv,
            device_id=to,
            device_id_type=MESH,
        )

    inner = pl.ds(COLS, CELLS)
    half = [pl.ds(f * CELLS, CELLS) for f in range(2)]
    plane = [pl.ds(3 * dt, 3) for dt in range(3)]

    moves = (
        [(lat_ref.at[half[f]], xb.at[2 + f, inner]) for f in (1, 0)]
        + [(w1_ref.at[plane[dt]], w1.at[plane[dt]]) for dt in (2, 1, 0)]
        + [
            (place_ref, place),
            (table_ref, table),
            (side_ref, side),
            (gain_ref, gain),
            (shift_ref, shift),
            (wq_ref, wq),
            (wk_ref, wk),
            (wv_ref, wv),
            (wo_ref, wo),
            (w2_ref, w2),
        ]
    )
    loads = [pltpu.make_async_copy(src, dst, lsem.at[i]) for i, (src, dst) in enumerate(moves)]
    for copy in loads[:5]:
        copy.start()

    barrier = pltpu.get_barrier_semaphore()
    greeted = [later(tms - 1), later(1)]
    greeted += [(c, t) for c in (cam_above, cam_below) for t in (tm, pair)]
    greeted += [later(i) for i in range(2, tms - 1)]
    if tms == 2:
        greeted = greeted[1:]
    for to in greeted:
        pl.semaphore_signal(barrier, inc=1, device_id=to, device_id_type=MESH)
    pl.semaphore_wait(barrier, len(greeted))

    halo = [
        remote(lat_ref.at[half[f]], xb.at[f, inner], hsend.at[f], hrecv.at[f], after)
        for f in range(2)
    ]

    @pl.when(jnp.logical_not(is_last))
    def _():
        halo[1].start()
        halo[0].start()

    for copy in loads[5:]:
        copy.start()
    zero = jnp.zeros((COLS, CHANS), BF16)
    for slot in range(4):
        for at in (0, COLS + CELLS):
            xb[slot, pl.ds(at, COLS), :] = zero
            mb[slot, pl.ds(at, COLS), :] = zero
    for copy in loads[:3]:
        copy.wait()
    first[half[0], :] = conv_terms(xb, w1, [(2, 2)])
    loads[3].wait()
    first[half[1], :] = conv_terms(xb, w1, [(3, 2), (2, 1)])
    loads[4].wait()

    @pl.when(is_first)
    def _():
        xb[0, inner, :] = xb[2, inner, :]
        xb[1, inner, :] = xb[2, inner, :]

    @pl.when(jnp.logical_not(is_first))
    def _():
        halo[1].wait_recv()

    first[half[1], :] += conv_terms(xb, w1, [(1, 0)])

    means, squares = [None, None], [None, None]

    def measure(f):
        rows = first[half[f], :]
        means[f] = jnp.sum(rows, axis=0, keepdims=True) / CELLS
        dev = rows - means[f]
        squares[f] = jnp.sum(dev * dev, axis=0, keepdims=True)

    measure(1)

    @pl.when(jnp.logical_not(is_first))
    def _():
        halo[0].wait_recv()

    first[half[0], :] += conv_terms(xb, w1, [(0, 0), (1, 1)])
    measure(0)

    mean_here = 0.5 * (means[0] + means[1])
    gap = means[1] - means[0]
    st[0, 0:1, :] = mean_here
    st[0, 1:2, :] = squares[0] + squares[1] + (0.5 * CELLS) * (gap * gap)
    swaps = [
        remote(st.at[0], st.at[i], ssend.at[i - 1], srecv.at[i - 1], later(i))
        for i in range(1, tms)
    ]
    for copy in swaps:
        copy.start()

    sides_of = (cam_above, cam_below)
    early = [
        [
            remote(
                first.at[half[f]],
                far.at[n, half[f]],
                csend.at[2 * f + n],
                crecv.at[2 * f + n],
                (sides_of[n], tm),
            )
            for n in range(2)
        ]
        for f in range(2)
    ]
    late = [
        [
            remote(
                hid.at[half[f]],
                nbr.at[n, half[f]],
                csend.at[2 * f + n],
                crecv.at[2 * f + n],
                (sides_of[n], tm),
            )
            for n in range(2)
        ]
        for f in range(2)
    ]

    @pl.when(core == 1)
    def _():
        for f in (1, 0):
            for copy in early[f]:
                copy.start()

    row_group = lax.broadcasted_iota(jnp.int32, (CHANS, CHANS), 0) // (CHANS // GROUPS)
    col_group = lax.broadcasted_iota(jnp.int32, (CHANS, CHANS), 1) // (CHANS // GROUPS)
    same = (row_group == col_group).astype(F32)

    def group_sum(row):
        wide = jnp.broadcast_to(row, (8, CHANS))
        return jnp.dot(
            wide, same, precision=lax.Precision.HIGHEST, preferred_element_type=F32
        )[0:1]

    for copy in loads[5:]:
        copy.wait()
    ids = lax.broadcasted_iota(jnp.int32, (cams, CHANS), 0)
    my_place = place[cam]
    below_place = place[cam_below]
    below_is_left = below_place == lax.rem(my_place + cams - 1, cams)
    table_row = jnp.sum(jnp.where(ids == my_place, table[...], 0.0), axis=0, keepdims=True)
    extra = jnp.dot(
        jnp.broadcast_to(table_row, (8, CHANS)),
        wq[...].astype(F32),
        precision=lax.Precision.HIGHEST,
        preferred_element_type=F32,
    )[0:1]
    sides = side[...].astype(F32)
    side_below = jnp.where(below_is_left, sides[0:1], sides[1:2])
    side_above = jnp.where(below_is_left, sides[1:2], sides[0:1])
    side_wide = jnp.concatenate(
        [
            jnp.broadcast_to(side_below, (128, CHANS)),
            jnp.broadcast_to(side_above, (128, CHANS)),
        ],
        axis=0,
    ).astype(BF16)

    for copy in swaps:
        copy.wait()
    cells = 2 * CELLS
    every = st[:, 0, :]
    mean_chan = jnp.sum(every, axis=0, keepdims=True) / tms
    away = every - mean_chan
    m2_chan = jnp.sum(st[:, 1, :], axis=0, keepdims=True) + cells * jnp.sum(
        away * away, axis=0, keepdims=True
    )
    per_group = CHANS // GROUPS
    mean = group_sum(mean_chan) / per_group
    away = mean_chan - mean
    spread = group_sum(m2_chan + (cells * tms) * (away * away)) / (per_group * cells * tms)
    scale = lax.rsqrt(spread + 1e-05) * gain[...]
    fw[0:1, :] = mean
    fw[1:2, :] = scale
    forwards = [
        remote(fw, fw_in.at[n], fsend.at[n], frecv.at[n], (sides_of[n], pair)) for n in range(2)
    ]

    @pl.when(core == 0)
    def _():
        for copy in forwards:
            copy.start()

    def silu(v):
        return (v / (1.0 + jnp.exp(-v))).astype(BF16)

    for f in (1, 0):
        hid[half[f], :] = silu((first[half[f], :] - mean) * scale + shift[...])

        @pl.when(core == 0)
        def _():
            for copy in late[f]:
                copy.start()

    for f in (1, 0):
        query[half[f], :] = (dot(hid[half[f], :], wq[...]) + extra).astype(BF16)

    mixed_halo = [
        remote(mb.at[2 + f, inner], mb.at[f, inner], msend.at[f], mrecv.at[f], after)
        for f in range(2)
    ]

    @pl.when(core == 1)
    def _():
        for copy in forwards:
            copy.wait_recv()

    for f in (1, 0):
        q = query[half[f], :]
        tilt = dot_t(q, side_wide)
        bias = [tilt[:, 0:1], tilt[:, 128:129]]
        scores, values = [], []

        @pl.when(core == 1)
        def _():
            for n in range(2):
                early[f][n].wait_recv()
                nbr[n, half[f], :] = silu(
                    (far[n, half[f], :] - fw_in[n, 0:1, :]) * fw_in[n, 1:2, :] + shift[...]
                )

        @pl.when(core == 0)
        def _():
            for n in range(2):
                late[f][n].wait_recv()

        for n in range(2):
            rows = nbr[n, half[f], :]
            keys = dot(rows, wk[...]).astype(BF16)
            values.append(dot(rows, wv[...]).astype(BF16))
            scores.append((dot_t(q, keys) + bias[n]) * CHANS ** (-0.5))
        top = jnp.maximum(
            jnp.max(scores[0], axis=1, keepdims=True), jnp.max(scores[1], axis=1, keepdims=True)
        )
        expo = [jnp.exp(s - top) for s in scores]
        total = jnp.sum(expo[0], axis=1, keepdims=True) + jnp.sum(expo[1], axis=1, keepdims=True)
        inverse = 1.0 / total
        attended = (
            dot((expo[0] * inverse).astype(BF16), values[0])
            + dot((expo[1] * inverse).astype(BF16), values[1])
        ).astype(BF16)
        mixed = hid[half[f], :].astype(F32) + dot(attended, wo[...])
        mb[2 + f, inner, :] = mixed.astype(BF16)

        @pl.when(jnp.logical_not(is_last))
        def _():
            mixed_halo[f].start()

    part[half[0], :] = conv_terms(mb, w2, [(2, 2)])
    part[half[1], :] = conv_terms(mb, w2, [(3, 2), (2, 1)])

    @pl.when(is_first)
    def _():
        mb[0, inner, :] = mb[2, inner, :]
        mb[1, inner, :] = mb[2, inner, :]

    @pl.when(jnp.logical_not(is_first))
    def _():
        mixed_halo[1].wait_recv()

    total = part[half[1], :] + conv_terms(mb, w2, [(1, 0)])
    out_ref[half[1], :] = (xb[3, inner, :].astype(F32) + total).astype(BF16)

    @pl.when(jnp.logical_not(is_first))
    def _():
        mixed_halo[0].wait_recv()

    total = part[half[0], :] + conv_terms(mb, w2, [(0, 0), (1, 1)])
    out_ref[half[0], :] = (xb[2, inner, :].astype(F32) + total).astype(BF16)

    @pl.when(core == 1)
    def _():
        for f in range(2):
            for copy in early[f]:
                copy.wait_send()

    @pl.when(core == 0)
    def _():
        for f in range(2):
            for copy in late[f]:
                copy.wait_send()
        for copy in forwards:
            copy.wait_send()

    @pl.when(jnp.logical_not(is_last))
    def _():
        for f in range(2):
            halo[f].wait_send()
            mixed_halo[f].wait_send()


def on_device(
    latents,
    cycle_position,
    conv_first,
    conv_second,
    norm_gain,
    norm_shift,
    w_query,
    w_key,
    w_value,
    w_out,
    camera_table,
    side_embed,
):
    cams, tms = lax.axis_size("cam"), lax.axis_size("tm")
    shape = latents.shape
    vmem = pl.BlockSpec(memory_space=pltpu.VMEM)
    hbm = pl.BlockSpec(memory_space=pltpu.HBM)
    dma = pltpu.SemaphoreType.DMA
    flops = 2 * 1024 * 256 * 256 * (54 + 6) + 4 * 1024 * 1024 * 256
    out = pl.pallas_call(
        functools.partial(block_kernel, cams, tms),
        out_shape=jax.ShapeDtypeStruct((2 * CELLS, CHANS), BF16),
        in_specs=[hbm] * 12,
        out_specs=vmem,
        scratch_shapes=[
            pltpu.VMEM((4, TALL, CHANS), BF16),
            pltpu.VMEM((4, TALL, CHANS), BF16),
            pltpu.VMEM((9, 3 * CHANS, CHANS), BF16),
            pltpu.VMEM((9, 3 * CHANS, CHANS), BF16),
            pltpu.VMEM((2 * CELLS, CHANS), F32),
            pltpu.VMEM((2 * CELLS, CHANS), F32),
            pltpu.VMEM((2, 2 * CELLS, CHANS), F32),
            pltpu.VMEM((2, 2 * CELLS, CHANS), BF16),
            pltpu.VMEM((2 * CELLS, CHANS), BF16),
            pltpu.VMEM((2 * CELLS, CHANS), BF16),
            pltpu.VMEM((tms, 2, CHANS), F32),
            pltpu.VMEM((2, CHANS), F32),
            pltpu.VMEM((2, 2, CHANS), F32),
            pltpu.SMEM((cams,), jnp.int32),
            pltpu.VMEM((1, CHANS), F32),
            pltpu.VMEM((1, CHANS), F32),
        ]
        + [pltpu.VMEM((CHANS, CHANS), BF16)] * 4
        + [
            pltpu.VMEM((cams, CHANS), F32),
            pltpu.VMEM((2, CHANS), BF16),
            dma((15,)),
            dma((2,)),
            dma((2,)),
            dma((tms - 1,)),
            dma((tms - 1,)),
            dma((4,)),
            dma((4,)),
            dma((2,)),
            dma((2,)),
            dma((2,)),
            dma((2,)),
        ],
        compiler_params=pltpu.CompilerParams(
            collective_id=0, has_side_effects=True, vmem_limit_bytes=62 * 2**20
        ),
        cost_estimate=pl.CostEstimate(
            flops=flops, bytes_accessed=9 * 2**20, transcendentals=2**20
        ),
    )(
        latents.reshape(2 * CELLS, CHANS),
        cycle_position,
        conv_first.reshape(9, 3 * CHANS, CHANS),
        conv_second.reshape(9, 3 * CHANS, CHANS),
        norm_gain.reshape(1, CHANS),
        norm_shift.reshape(1, CHANS),
        w_query,
        w_key,
        w_value,
        w_out,
        camera_table,
        side_embed,
    )
    return out.reshape(shape)


def solution(mesh):
    in_specs = (P("cam", "tm", None, None, None),) + (P(),) * 11
    out_specs = P("cam", "tm", None, None, None)
    return jax.shard_map(
        on_device, mesh=mesh, in_specs=in_specs, out_specs=out_specs, check_vma=False
    )
```

time: 218 us -> 52.6 us (0.24)
  the two profiles are of different devices: /device:TPU:128 before, /device:TPU:36 now
where the time goes in v1:
time: 52.6 us; the launch traced here: 52.4 us
  Pallas kernels  50.6 us (96%)
  local copies, waits for them, and re-layouts  1.87 us (4%)
    pallas_call x1, Pallas kernels, on_device(): pl.pallas_call(functools.partial(block_kernel, cams, tms), out_shape=jax....  50.6 us
    unnamed x1, local copies, waits for them, and re-layouts  1.87 us

profile of v1, /device:TPU:36, one launch (start us, length us, event | category | flops | bytes accessed | tf_op | source)
XLA Modules:
  0.0 52.4 jit_solution(12814149648137688232)
XLA Ops:
  0.0 50.6 %shard_map.118 = bf16[1024,256]{1,0:T(8,128)(2,1)} custom-call(bf16[1024,256]{1,0:T(8,128)(2,1)} %bitcast.9, s32[8]{0:T(128)} %place_ref.1, bf16[9,768,256]{2,1,0:T(8,128)(2,1)} %bitcast.7, bf16[9,768,256]{2,1,0:T(8,128)(2,1)} %bitcast.8, f32[1,256]{1,0:T(1,128)} %bitcast.10, f32[1,256]{1,0:T(1,128)} %bitcast.11, bf16[256,256]{1,0:T(8,128)(2,1)} %wq_ref.1, ...), custom_call_target="tpu_custom_call" | custom-call | flops 9126805504 | bytes 9437184 | tf_op jit(solution)/shard_map/pallas_call | solution.py:435
  50.6 1.9 %copy.14 = bf16[1,2,16,32,256]{4,3,2,1,0:T(8,128)(2,1)} copy(bf16[1,2,16,32,256]{4,3,2,1,0:T(8,128)(2,1)} %bitcast.6) | data formatting | bytes 1048576

commit v2 on v1

--- a/solution.py
+++ b/solution.py
@@ -14,6 +14,7 @@
 ROWS, COLS, CHANS = 16, 32, 256
 CELLS = ROWS * COLS
 TALL = CELLS + 2 * COLS
+SPLIT = 256
 
 
 def dot(a, b):
@@ -67,6 +68,8 @@
     nbr,
     hid,
     query,
+    own,
+    mate,
     st,
     fw,
     fw_in,
@@ -82,6 +85,7 @@
     lsem,
     hsend,
     hrecv,
+    psem,
     ssend,
     srecv,
     csend,
@@ -98,6 +102,8 @@
     core = lax.rem(tm, 2)
     pair = tm + 1 - 2 * core
     after = (cam, lax.rem(tm + 1, tms))
+    sides_of = (cam_above, cam_below)
+    chips = tms // 2
     is_first = tm == 0
     is_last = tm == tms - 1
 
@@ -139,24 +145,41 @@
         copy.start()
 
     barrier = pltpu.get_barrier_semaphore()
-    greeted = [later(tms - 1), later(1)]
-    greeted += [(c, t) for c in (cam_above, cam_below) for t in (tm, pair)]
-    greeted += [later(i) for i in range(2, tms - 1)]
-    if tms == 2:
-        greeted = greeted[1:]
-    for to in greeted:
+
+    def greet(to):
         pl.semaphore_signal(barrier, inc=1, device_id=to, device_id_type=MESH)
-    pl.semaphore_wait(barrier, len(greeted))
 
     halo = [
         remote(lat_ref.at[half[f]], xb.at[f, inner], hsend.at[f], hrecv.at[f], after)
         for f in range(2)
     ]
 
+    @pl.when(core == 0)
+    def _():
+        greet(later(tms - 1))
+        greet((cam, pair))
+        for c in sides_of:
+            greet((c, tm))
+        for i in range(1, chips):
+            greet(later(2 * i))
+        pl.semaphore_wait(barrier, tms + 1)
+
+    @pl.when(core == 1)
+    def _():
+        greet((cam, pair))
+        for c in sides_of:
+            greet((c, tm))
+        pl.semaphore_wait(barrier, 4)
+
     @pl.when(jnp.logical_not(is_last))
     def _():
         halo[1].start()
         halo[0].start()
+
+    @pl.when(core == 1)
+    def _():
+        for i in range(1, chips):
+            greet(later(2 * i + tms - 1))
 
     for copy in loads[5:]:
         copy.start()
@@ -193,67 +216,77 @@
 
     measure(1)
 
-    @pl.when(jnp.logical_not(is_first))
-    def _():
-        halo[0].wait_recv()
-
-    first[half[0], :] += conv_terms(xb, w1, [(0, 0), (1, 1)])
-    measure(0)
-
-    mean_here = 0.5 * (means[0] + means[1])
-    gap = means[1] - means[0]
-    st[0, 0:1, :] = mean_here
-    st[0, 1:2, :] = squares[0] + squares[1] + (0.5 * CELLS) * (gap * gap)
-    swaps = [
-        remote(st.at[0], st.at[i], ssend.at[i - 1], srecv.at[i - 1], later(i))
-        for i in range(1, tms)
-    ]
-    for copy in swaps:
-        copy.start()
-
-    sides_of = (cam_above, cam_below)
     early = [
         [
             remote(
-                first.at[half[f]],
-                far.at[n, half[f]],
-                csend.at[2 * f + n],
-                crecv.at[2 * f + n],
+                first.at[rows],
+                far.at[n, pl.ds(at, size)],
+                csend.at[2 * i + n],
+                crecv.at[2 * i + n],
                 (sides_of[n], tm),
             )
             for n in range(2)
         ]
-        for f in range(2)
+        for i, (at, size, rows) in enumerate(
+            (at, size, pl.ds(CELLS + at, size)) for at, size in ((0, SPLIT), (SPLIT, CELLS - SPLIT))
+        )
     ]
-    late = [
-        [
-            remote(
-                hid.at[half[f]],
-                nbr.at[n, half[f]],
-                csend.at[2 * f + n],
-                crecv.at[2 * f + n],
-                (sides_of[n], tm),
-            )
-            for n in range(2)
-        ]
-        for f in range(2)
-    ]
+
+    @pl.when(core == 0)
+    def _():
+        for copy in early[0]:
+            copy.start()
+
+    @pl.when(jnp.logical_not(is_first))
+    def _():
+        halo[0].wait_recv()
+
+    first[half[0], :] += conv_terms(xb, w1, [(0, 0), (1, 1)])
+    measure(0)
+
+    def joined(mean_a, mean_b, square_a, square_b, count):
+        gap = mean_b - mean_a
+        return 0.5 * (mean_a + mean_b), square_a + square_b + (0.5 * count) * (gap * gap)
+
+    mean_here, square_here = joined(means[0], means[1], squares[0], squares[1], CELLS)
+    hand = remote(own, mate, psem.at[0], psem.at[1], (cam, pair))
+    own[0:1, :] = mean_here
+    own[1:2, :] = square_here
+    swaps = [remote(st.at[0], st.at[0], ssend.at[0], srecv.at[0], (cam, pair))]
+    for i in range(1, chips):
+        swaps.append(remote(st.at[0], st.at[i], ssend.at[2 * i], srecv.at[i], later(2 * i)))
+    for i in range(1, chips):
+        swaps.append(remote(st.at[0], st.at[i], ssend.at[2 * i + 1], srecv.at[i], later(2 * i + 1)))
+
+    @pl.when(core == 0)
+    def _():
+        hand.wait_recv()
+        mean_chip, square_chip = joined(
+            mean_here, mate[0:1, :], square_here, mate[1:2, :], 2 * CELLS
+        )
+        st[0, 0:1, :] = mean_chip
+        st[0, 1:2, :] = square_chip
+        for copy in swaps:
+            copy.start()
+        for copy in early[1]:
+            copy.start()
 
     @pl.when(core == 1)
     def _():
-        for f in (1, 0):
-            for copy in early[f]:
+        hand.start()
+        for pieces in early:
+            for copy in pieces:
                 copy.start()
 
-    row_group = lax.broadcasted_iota(jnp.int32, (CHANS, CHANS), 0) // (CHANS // GROUPS)
-    col_group = lax.broadcasted_iota(jnp.int32, (CHANS, CHANS), 1) // (CHANS // GROUPS)
-    same = (row_group == col_group).astype(F32)
+    lane = lax.broadcasted_iota(jnp.int32, (8, CHANS), 1)
 
     def group_sum(row):
         wide = jnp.broadcast_to(row, (8, CHANS))
-        return jnp.dot(
-            wide, same, precision=lax.Precision.HIGHEST, preferred_element_type=F32
-        )[0:1]
+        for bit in (1, 2, 4):
+            wide += jnp.where(
+                lane & bit == 0, pltpu.roll(wide, CHANS - bit, 1), pltpu.roll(wide, bit, 1)
+            )
+        return wide[0:1]
 
     for copy in loads[5:]:
         copy.wait()
@@ -279,11 +312,15 @@
         axis=0,
     ).astype(BF16)
 
-    for copy in swaps:
-        copy.wait()
-    cells = 2 * CELLS
+    @pl.when(core == 1)
+    def _():
+        swaps[0].wait_recv()
+
+    for copy in swaps[1:chips]:
+        copy.wait_recv()
+    cells = 4 * CELLS
     every = st[:, 0, :]
-    mean_chan = jnp.sum(every, axis=0, keepdims=True) / tms
+    mean_chan = jnp.sum(every, axis=0, keepdims=True) / chips
     away = every - mean_chan
     m2_chan = jnp.sum(st[:, 1, :], axis=0, keepdims=True) + cells * jnp.sum(
         away * away, axis=0, keepdims=True
@@ -291,30 +328,30 @@
     per_group = CHANS // GROUPS
     mean = group_sum(mean_chan) / per_group
     away = mean_chan - mean
-    spread = group_sum(m2_chan + (cells * tms) * (away * away)) / (per_group * cells * tms)
+    spread = group_sum(m2_chan + (cells * chips) * (away * away)) / (
+        per_group * cells * chips
+    )
     scale = lax.rsqrt(spread + 1e-05) * gain[...]
     fw[0:1, :] = mean
     fw[1:2, :] = scale
     forwards = [
-        remote(fw, fw_in.at[n], fsend.at[n], frecv.at[n], (sides_of[n], pair)) for n in range(2)
+        remote(fw, fw_in.at[n], fsend.at[n], frecv.at[n], (sides_of[n], tm)) for n in range(2)
     ]
-
-    @pl.when(core == 0)
-    def _():
-        for copy in forwards:
-            copy.start()
+    for copy in forwards:
+        copy.start()
 
     def silu(v):
         return (v / (1.0 + jnp.exp(-v))).astype(BF16)
 
-    for f in (1, 0):
+    late = [
+        remote(hid.at[half[0]], nbr.at[n], csend.at[4 + n], crecv.at[4 + n], (sides_of[n], tm))
+        for n in range(2)
+    ]
+    for f in range(2):
         hid[half[f], :] = silu((first[half[f], :] - mean) * scale + shift[...])
-
-        @pl.when(core == 0)
-        def _():
-            for copy in late[f]:
+        if f == 0:
+            for copy in late:
                 copy.start()
-
     for f in (1, 0):
         query[half[f], :] = (dot(hid[half[f], :], wq[...]) + extra).astype(BF16)
 
@@ -323,10 +360,8 @@
         for f in range(2)
     ]
 
-    @pl.when(core == 1)
-    def _():
-        for copy in forwards:
-            copy.wait_recv()
+    for copy in forwards:
+        copy.wait_recv()
 
     for f in (1, 0):
         q = query[half[f], :]
@@ -334,21 +369,14 @@
         bias = [tilt[:, 0:1], tilt[:, 128:129]]
         scores, values = [], []
 
-        @pl.when(core == 1)
-        def _():
-            for n in range(2):
-                early[f][n].wait_recv()
-                nbr[n, half[f], :] = silu(
-                    (far[n, half[f], :] - fw_in[n, 0:1, :]) * fw_in[n, 1:2, :] + shift[...]
-                )
-
-        @pl.when(core == 0)
-        def _():
-            for n in range(2):
-                late[f][n].wait_recv()
-
         for n in range(2):
-            rows = nbr[n, half[f], :]
+            if f == 1:
+                early[0][n].wait_recv()
+                early[1][n].wait_recv()
+                rows = silu((far[n] - fw_in[n, 0:1, :]) * fw_in[n, 1:2, :] + shift[...])
+            else:
+                late[n].wait_recv()
+                rows = nbr[n]
             keys = dot(rows, wk[...]).astype(BF16)
             values.append(dot(rows, wv[...]).astype(BF16))
             scores.append((dot_t(q, keys) + bias[n]) * CHANS ** (-0.5))
@@ -391,19 +419,17 @@
     total = part[half[0], :] + conv_terms(mb, w2, [(0, 0), (1, 1)])
     out_ref[half[0], :] = (xb[2, inner, :].astype(F32) + total).astype(BF16)
 
+    for copy in early[0] + early[1] + late + forwards:
+        copy.wait_send()
+
+    @pl.when(core == 0)
+    def _():
+        for copy in swaps:
+            copy.wait_send()
+
     @pl.when(core == 1)
     def _():
-        for f in range(2):
-            for copy in early[f]:
-                copy.wait_send()
-
-    @pl.when(core == 0)
-    def _():
-        for f in range(2):
-            for copy in late[f]:
-                copy.wait_send()
-        for copy in forwards:
-            copy.wait_send()
+        hand.wait_send()
 
     @pl.when(jnp.logical_not(is_last))
     def _():
@@ -444,11 +470,13 @@
             pltpu.VMEM((9, 3 * CHANS, CHANS), BF16),
             pltpu.VMEM((2 * CELLS, CHANS), F32),
             pltpu.VMEM((2 * CELLS, CHANS), F32),
-            pltpu.VMEM((2, 2 * CELLS, CHANS), F32),
-            pltpu.VMEM((2, 2 * CELLS, CHANS), BF16),
+            pltpu.VMEM((2, CELLS, CHANS), F32),
+            pltpu.VMEM((2, CELLS, CHANS), BF16),
             pltpu.VMEM((2 * CELLS, CHANS), BF16),
             pltpu.VMEM((2 * CELLS, CHANS), BF16),
-            pltpu.VMEM((tms, 2, CHANS), F32),
+            pltpu.VMEM((2, CHANS), F32),
+            pltpu.VMEM((2, CHANS), F32),
+            pltpu.VMEM((tms // 2, 2, CHANS), F32),
             pltpu.VMEM((2, CHANS), F32),
             pltpu.VMEM((2, 2, CHANS), F32),
             pltpu.SMEM((cams,), jnp.int32),
@@ -462,10 +490,11 @@
             dma((15,)),
             dma((2,)),
             dma((2,)),
-            dma((tms - 1,)),
-            dma((tms - 1,)),
-            dma((4,)),
-            dma((4,)),
+            dma((2,)),
+            dma((tms,)),
+            dma((tms // 2,)),
+            dma((6,)),
+            dma((6,)),
             dma((2,)),
             dma((2,)),
             dma((2,)),

time: 52.6 us -> 52.2 us (level)
  the two profiles are of different devices: /device:TPU:36 before, /device:TPU:64 now
where the time goes in v2:
time: 52.2 us; the launch traced here: 52.1 us
  Pallas kernels  50.2 us (96%)
  local copies, waits for them, and re-layouts  1.87 us (4%)
    pallas_call x1, Pallas kernels, on_device(): pl.pallas_call(functools.partial(block_kernel, cams, tms), out_shape=jax....  50.2 us
    unnamed x1, local copies, waits for them, and re-layouts  1.87 us

profile of v2, /device:TPU:64, one launch (start us, length us, event | category | flops | bytes accessed | tf_op | source)
XLA Modules:
  0.0 52.1 jit_solution(5665868144932761323)
XLA Ops:
  0.0 50.2 %shard_map.118 = bf16[1024,256]{1,0:T(8,128)(2,1)} custom-call(bf16[1024,256]{1,0:T(8,128)(2,1)} %bitcast.9, s32[8]{0:T(128)} %place_ref.1, bf16[9,768,256]{2,1,0:T(8,128)(2,1)} %bitcast.7, bf16[9,768,256]{2,1,0:T(8,128)(2,1)} %bitcast.8, f32[1,256]{1,0:T(1,128)} %bitcast.10, f32[1,256]{1,0:T(1,128)} %bitcast.11, bf16[256,256]{1,0:T(8,128)(2,1)} %wq_ref.1, ...), custom_call_target="tpu_custom_call" | custom-call | flops 9126805504 | bytes 9437184 | tf_op jit(solution)/shard_map/pallas_call | solution.py:461
  50.2 1.9 %copy.14 = bf16[1,2,16,32,256]{4,3,2,1,0:T(8,128)(2,1)} copy(bf16[1,2,16,32,256]{4,3,2,1,0:T(8,128)(2,1)} %bitcast.6) | data formatting | bytes 1048576

commit v3 on v2

--- a/solution.py
+++ b/solution.py
@@ -14,7 +14,7 @@
 ROWS, COLS, CHANS = 16, 32, 256
 CELLS = ROWS * COLS
 TALL = CELLS + 2 * COLS
-SPLIT = 256
+SPAN = 85.0
 
 
 def dot(a, b):
@@ -64,7 +64,7 @@
     w2,
     first,
     part,
-    far,
+    code,
     nbr,
     hid,
     query,
@@ -160,6 +160,7 @@
         greet((cam, pair))
         for c in sides_of:
             greet((c, tm))
+            greet((c, pair))
         for i in range(1, chips):
             greet(later(2 * i))
         pl.semaphore_wait(barrier, tms + 1)
@@ -169,7 +170,7 @@
         greet((cam, pair))
         for c in sides_of:
             greet((c, tm))
-        pl.semaphore_wait(barrier, 4)
+        pl.semaphore_wait(barrier, 6)
 
     @pl.when(jnp.logical_not(is_last))
     def _():
@@ -205,6 +206,7 @@
         halo[1].wait_recv()
 
     first[half[1], :] += conv_terms(xb, w1, [(1, 0)])
+    first[half[0], :] += conv_terms(xb, w1, [(1, 1)])
 
     means, squares = [None, None], [None, None]
 
@@ -216,32 +218,11 @@
 
     measure(1)
 
-    early = [
-        [
-            remote(
-                first.at[rows],
-                far.at[n, pl.ds(at, size)],
-                csend.at[2 * i + n],
-                crecv.at[2 * i + n],
-                (sides_of[n], tm),
-            )
-            for n in range(2)
-        ]
-        for i, (at, size, rows) in enumerate(
-            (at, size, pl.ds(CELLS + at, size)) for at, size in ((0, SPLIT), (SPLIT, CELLS - SPLIT))
-        )
-    ]
-
-    @pl.when(core == 0)
-    def _():
-        for copy in early[0]:
-            copy.start()
-
     @pl.when(jnp.logical_not(is_first))
     def _():
         halo[0].wait_recv()
 
-    first[half[0], :] += conv_terms(xb, w1, [(0, 0), (1, 1)])
+    first[half[0], :] += conv_terms(xb, w1, [(0, 0)])
     measure(0)
 
     def joined(mean_a, mean_b, square_a, square_b, count):
@@ -257,6 +238,7 @@
         swaps.append(remote(st.at[0], st.at[i], ssend.at[2 * i], srecv.at[i], later(2 * i)))
     for i in range(1, chips):
         swaps.append(remote(st.at[0], st.at[i], ssend.at[2 * i + 1], srecv.at[i], later(2 * i + 1)))
+    far_first = sorted(range(1, chips), key=lambda i: abs(2 * i - chips))
 
     @pl.when(core == 0)
     def _():
@@ -266,17 +248,37 @@
         )
         st[0, 0:1, :] = mean_chip
         st[0, 1:2, :] = square_chip
-        for copy in swaps:
+        for i in far_first:
+            swaps[i].start()
+            swaps[i + chips - 1].start()
+        swaps[0].start()
+
+    @pl.when(core == 1)
+    def _():
+        hand.start()
+
+    cam_copies = [None, None]
+    for f in (1, 0):
+        rows = first[half[f], :]
+        code[f, pl.ds(CELLS, 16), :] = jnp.broadcast_to(means[f], (16, CHANS)).astype(BF16)
+        high = code[f, pl.ds(CELLS, 16), :].astype(F32)[0:1]
+        code[f, pl.ds(CELLS + 16, 16), :] = jnp.broadcast_to(means[f] - high, (16, CHANS)).astype(
+            BF16
+        )
+        rows = rows - (high + code[f, pl.ds(CELLS + 16, 16), :].astype(F32)[0:1])
+        reach = jnp.max(jnp.abs(rows), axis=0, keepdims=True)
+        step = jnp.maximum(reach * (1.01 / SPAN), 1e-30)
+        code[f, pl.ds(CELLS + 32, 16), :] = jnp.broadcast_to(step, (16, CHANS)).astype(BF16)
+        step = code[f, pl.ds(CELLS + 32, 16), :].astype(F32)[0:1]
+        code[f, pl.ds(0, CELLS), :] = jnp.exp(rows * (1.0 / step)).astype(BF16)
+        cam_copies[f] = [
+            remote(
+                code.at[f], nbr.at[n, f], csend.at[2 * f + n], crecv.at[2 * f + n], (sides_of[n], tm)
+            )
+            for n in range(2)
+        ]
+        for copy in cam_copies[f]:
             copy.start()
-        for copy in early[1]:
-            copy.start()
-
-    @pl.when(core == 1)
-    def _():
-        hand.start()
-        for pieces in early:
-            for copy in pieces:
-                copy.start()
 
     lane = lax.broadcasted_iota(jnp.int32, (8, CHANS), 1)
 
@@ -335,23 +337,21 @@
     fw[0:1, :] = mean
     fw[1:2, :] = scale
     forwards = [
-        remote(fw, fw_in.at[n], fsend.at[n], frecv.at[n], (sides_of[n], tm)) for n in range(2)
+        remote(fw, fw_in.at[n], fsend.at[2 * n + i], frecv.at[n], (sides_of[n], t))
+        for n in range(2)
+        for i, t in enumerate((tm, pair))
     ]
-    for copy in forwards:
-        copy.start()
+
+    @pl.when(core == 1)
+    def _():
+        for copy in forwards:
+            copy.start()
 
     def silu(v):
         return (v / (1.0 + jnp.exp(-v))).astype(BF16)
 
-    late = [
-        remote(hid.at[half[0]], nbr.at[n], csend.at[4 + n], crecv.at[4 + n], (sides_of[n], tm))
-        for n in range(2)
-    ]
-    for f in range(2):
+    for f in (1, 0):
         hid[half[f], :] = silu((first[half[f], :] - mean) * scale + shift[...])
-        if f == 0:
-            for copy in late:
-                copy.start()
     for f in (1, 0):
         query[half[f], :] = (dot(hid[half[f], :], wq[...]) + extra).astype(BF16)
 
@@ -360,8 +360,8 @@
         for f in range(2)
     ]
 
-    for copy in forwards:
-        copy.wait_recv()
+    for n in range(2):
+        forwards[2 * n].wait_recv()
 
     for f in (1, 0):
         q = query[half[f], :]
@@ -370,13 +370,12 @@
         scores, values = [], []
 
         for n in range(2):
-            if f == 1:
-                early[0][n].wait_recv()
-                early[1][n].wait_recv()
-                rows = silu((far[n] - fw_in[n, 0:1, :]) * fw_in[n, 1:2, :] + shift[...])
-            else:
-                late[n].wait_recv()
-                rows = nbr[n]
+            cam_copies[f][n].wait_recv()
+            tag = nbr[n, f, pl.ds(CELLS, 48), :].astype(F32)
+            scale_there = fw_in[n, 1:2, :]
+            factor = tag[32:33] * scale_there
+            offset = ((tag[0:1] + tag[16:17]) - fw_in[n, 0:1, :]) * scale_there + shift[...]
+            rows = silu(jnp.log(nbr[n, f, pl.ds(0, CELLS), :].astype(F32)) * factor + offset)
             keys = dot(rows, wk[...]).astype(BF16)
             values.append(dot(rows, wv[...]).astype(BF16))
             scores.append((dot_t(q, keys) + bias[n]) * CHANS ** (-0.5))
@@ -411,16 +410,18 @@
 
     total = part[half[1], :] + conv_terms(mb, w2, [(1, 0)])
     out_ref[half[1], :] = (xb[3, inner, :].astype(F32) + total).astype(BF16)
+    part[half[0], :] += conv_terms(mb, w2, [(1, 1)])
 
     @pl.when(jnp.logical_not(is_first))
     def _():
         mixed_halo[0].wait_recv()
 
-    total = part[half[0], :] + conv_terms(mb, w2, [(0, 0), (1, 1)])
+    total = part[half[0], :] + conv_terms(mb, w2, [(0, 0)])
     out_ref[half[0], :] = (xb[2, inner, :].astype(F32) + total).astype(BF16)
 
-    for copy in early[0] + early[1] + late + forwards:
-        copy.wait_send()
+    for f in range(2):
+        for copy in cam_copies[f]:
+            copy.wait_send()
 
     @pl.when(core == 0)
     def _():
@@ -430,6 +431,8 @@
     @pl.when(core == 1)
     def _():
         hand.wait_send()
+        for copy in forwards:
+            copy.wait_send()
 
     @pl.when(jnp.logical_not(is_last))
     def _():
@@ -470,8 +473,8 @@
             pltpu.VMEM((9, 3 * CHANS, CHANS), BF16),
             pltpu.VMEM((2 * CELLS, CHANS), F32),
             pltpu.VMEM((2 * CELLS, CHANS), F32),
-            pltpu.VMEM((2, CELLS, CHANS), F32),
-            pltpu.VMEM((2, CELLS, CHANS), BF16),
+            pltpu.VMEM((2, CELLS + 48, CHANS), BF16),
+            pltpu.VMEM((2, 2, CELLS + 48, CHANS), BF16),
             pltpu.VMEM((2 * CELLS, CHANS), BF16),
             pltpu.VMEM((2 * CELLS, CHANS), BF16),
             pltpu.VMEM((2, CHANS), F32),
@@ -493,9 +496,9 @@
             dma((2,)),
             dma((tms,)),
             dma((tms // 2,)),
-            dma((6,)),
-            dma((6,)),
-            dma((2,)),
+            dma((4,)),
+            dma((4,)),
+            dma((4,)),
             dma((2,)),
             dma((2,)),
             dma((2,)),

time: 52.2 us -> 46.3 us (0.89)
  the two profiles are of different devices: /device:TPU:64 before, /device:TPU:32 now
where the time goes in v3:
time: 46.3 us; the launch traced here: 46.1 us
  Pallas kernels  44.3 us (96%)
  local copies, waits for them, and re-layouts  1.87 us (4%)
    pallas_call x1, Pallas kernels, on_device(): pl.pallas_call(functools.partial(block_kernel, cams, tms), out_shape=jax....  44.3 us
    unnamed x1, local copies, waits for them, and re-layouts  1.87 us

profile of v3, /device:TPU:32, one launch (start us, length us, event | category | flops | bytes accessed | tf_op | source)
XLA Modules:
  0.0 46.1 jit_solution(17644568771190959244)
XLA Ops:
  0.0 44.3 %shard_map.118 = bf16[1024,256]{1,0:T(8,128)(2,1)} custom-call(bf16[1024,256]{1,0:T(8,128)(2,1)} %bitcast.9, s32[8]{0:T(128)} %place_ref.1, bf16[9,768,256]{2,1,0:T(8,128)(2,1)} %bitcast.7, bf16[9,768,256]{2,1,0:T(8,128)(2,1)} %bitcast.8, f32[1,256]{1,0:T(1,128)} %bitcast.10, f32[1,256]{1,0:T(1,128)} %bitcast.11, bf16[256,256]{1,0:T(8,128)(2,1)} %wq_ref.1, ...), custom_call_target="tpu_custom_call" | custom-call | flops 9126805504 | bytes 9437184 | tf_op jit(solution)/shard_map/pallas_call | solution.py:464
  44.3 1.9 %copy.14 = bf16[1,2,16,32,256]{4,3,2,1,0:T(8,128)(2,1)} copy(bf16[1,2,16,32,256]{4,3,2,1,0:T(8,128)(2,1)} %bitcast.6) | data formatting | bytes 1048576

commit v4 on v3

--- a/solution.py
+++ b/solution.py
@@ -15,6 +15,9 @@
 CELLS = ROWS * COLS
 TALL = CELLS + 2 * COLS
 SPAN = 85.0
+CUT = 256
+TILE = 256
+SCORE = 1.4426950408889634 / 16.0
 
 
 def dot(a, b):
@@ -145,6 +148,7 @@
         copy.start()
 
     barrier = pltpu.get_barrier_semaphore()
+    far_first = sorted(range(1, chips), key=lambda i: abs(2 * i - chips))
 
     def greet(to):
         pl.semaphore_signal(barrier, inc=1, device_id=to, device_id_type=MESH)
@@ -161,7 +165,7 @@
         for c in sides_of:
             greet((c, tm))
             greet((c, pair))
-        for i in range(1, chips):
+        for i in far_first:
             greet(later(2 * i))
         pl.semaphore_wait(barrier, tms + 1)
 
@@ -170,6 +174,8 @@
         greet((cam, pair))
         for c in sides_of:
             greet((c, tm))
+        for i in far_first:
+            greet(later(2 * i + tms - 1))
         pl.semaphore_wait(barrier, 6)
 
     @pl.when(jnp.logical_not(is_last))
@@ -177,12 +183,7 @@
         halo[1].start()
         halo[0].start()
 
-    @pl.when(core == 1)
-    def _():
-        for i in range(1, chips):
-            greet(later(2 * i + tms - 1))
-
-    for copy in loads[5:]:
+    for copy in loads[5:14]:
         copy.start()
     zero = jnp.zeros((COLS, CHANS), BF16)
     for slot in range(4):
@@ -216,49 +217,7 @@
         dev = rows - means[f]
         squares[f] = jnp.sum(dev * dev, axis=0, keepdims=True)
 
-    measure(1)
-
-    @pl.when(jnp.logical_not(is_first))
-    def _():
-        halo[0].wait_recv()
-
-    first[half[0], :] += conv_terms(xb, w1, [(0, 0)])
-    measure(0)
-
-    def joined(mean_a, mean_b, square_a, square_b, count):
-        gap = mean_b - mean_a
-        return 0.5 * (mean_a + mean_b), square_a + square_b + (0.5 * count) * (gap * gap)
-
-    mean_here, square_here = joined(means[0], means[1], squares[0], squares[1], CELLS)
-    hand = remote(own, mate, psem.at[0], psem.at[1], (cam, pair))
-    own[0:1, :] = mean_here
-    own[1:2, :] = square_here
-    swaps = [remote(st.at[0], st.at[0], ssend.at[0], srecv.at[0], (cam, pair))]
-    for i in range(1, chips):
-        swaps.append(remote(st.at[0], st.at[i], ssend.at[2 * i], srecv.at[i], later(2 * i)))
-    for i in range(1, chips):
-        swaps.append(remote(st.at[0], st.at[i], ssend.at[2 * i + 1], srecv.at[i], later(2 * i + 1)))
-    far_first = sorted(range(1, chips), key=lambda i: abs(2 * i - chips))
-
-    @pl.when(core == 0)
-    def _():
-        hand.wait_recv()
-        mean_chip, square_chip = joined(
-            mean_here, mate[0:1, :], square_here, mate[1:2, :], 2 * CELLS
-        )
-        st[0, 0:1, :] = mean_chip
-        st[0, 1:2, :] = square_chip
-        for i in far_first:
-            swaps[i].start()
-            swaps[i + chips - 1].start()
-        swaps[0].start()
-
-    @pl.when(core == 1)
-    def _():
-        hand.start()
-
-    cam_copies = [None, None]
-    for f in (1, 0):
+    def encode(f):
         rows = first[half[f], :]
         code[f, pl.ds(CELLS, 16), :] = jnp.broadcast_to(means[f], (16, CHANS)).astype(BF16)
         high = code[f, pl.ds(CELLS, 16), :].astype(F32)[0:1]
@@ -271,14 +230,72 @@
         code[f, pl.ds(CELLS + 32, 16), :] = jnp.broadcast_to(step, (16, CHANS)).astype(BF16)
         step = code[f, pl.ds(CELLS + 32, 16), :].astype(F32)[0:1]
         code[f, pl.ds(0, CELLS), :] = jnp.exp(rows * (1.0 / step)).astype(BF16)
-        cam_copies[f] = [
+
+    pieces = [(1, pl.ds(0, CUT)), (1, pl.ds(CUT, CELLS + 48 - CUT)), (0, pl.ds(0, CELLS + 48))]
+    cam_copies = [
+        [
             remote(
-                code.at[f], nbr.at[n, f], csend.at[2 * f + n], crecv.at[2 * f + n], (sides_of[n], tm)
+                code.at[f, rows],
+                nbr.at[n, f, rows],
+                csend.at[2 * i + n],
+                crecv.at[2 * i + n],
+                (sides_of[n], tm),
             )
             for n in range(2)
         ]
-        for copy in cam_copies[f]:
+        for i, (f, rows) in enumerate(pieces)
+    ]
+
+    def send_code(i):
+        for copy in cam_copies[i]:
             copy.start()
+
+    measure(1)
+
+
+    @pl.when(jnp.logical_not(is_first))
+    def _():
+        halo[0].wait_recv()
+
+    first[half[0], :] += conv_terms(xb, w1, [(0, 0)])
+    measure(0)
+
+    def joined(mean_a, mean_b, square_a, square_b, count):
+        gap = mean_b - mean_a
+        return 0.5 * (mean_a + mean_b), square_a + square_b + (0.5 * count) * (gap * gap)
+
+    mean_here, square_here = joined(means[0], means[1], squares[0], squares[1], CELLS)
+    hand = remote(own, mate, psem.at[0], psem.at[1], (cam, pair))
+    own[0:1, :] = mean_here
+    own[1:2, :] = square_here
+    swaps = [remote(st.at[0], st.at[0], ssend.at[0], srecv.at[0], (cam, pair))]
+    for i in range(1, chips):
+        swaps.append(remote(st.at[0], st.at[i], ssend.at[2 * i], srecv.at[i], later(2 * i)))
+    for i in range(1, chips):
+        swaps.append(remote(st.at[0], st.at[i], ssend.at[2 * i + 1], srecv.at[i], later(2 * i + 1)))
+
+    @pl.when(core == 0)
+    def _():
+        hand.wait_recv()
+        mean_chip, square_chip = joined(
+            mean_here, mate[0:1, :], square_here, mate[1:2, :], 2 * CELLS
+        )
+        st[0, 0:1, :] = mean_chip
+        st[0, 1:2, :] = square_chip
+        for i in far_first:
+            swaps[i].start()
+            swaps[i + chips - 1].start()
+        swaps[0].start()
+
+    @pl.when(core == 1)
+    def _():
+        hand.start()
+
+    encode(1)
+    send_code(0)
+    send_code(1)
+    encode(0)
+    send_code(2)
 
     lane = lax.broadcasted_iota(jnp.int32, (8, CHANS), 1)
 
@@ -290,7 +307,8 @@
             )
         return wide[0:1]
 
-    for copy in loads[5:]:
+    loads[14].start()
+    for copy in loads[5:14]:
         copy.wait()
     ids = lax.broadcasted_iota(jnp.int32, (cams, CHANS), 0)
     my_place = place[cam]
@@ -348,7 +366,8 @@
             copy.start()
 
     def silu(v):
-        return (v / (1.0 + jnp.exp(-v))).astype(BF16)
+        h = 0.5 * v
+        return (h + h * jnp.tanh(h)).astype(BF16)
 
     for f in (1, 0):
         hid[half[f], :] = silu((first[half[f], :] - mean) * scale + shift[...])
@@ -356,46 +375,59 @@
         query[half[f], :] = (dot(hid[half[f], :], wq[...]) + extra).astype(BF16)
 
     mixed_halo = [
-        remote(mb.at[2 + f, inner], mb.at[f, inner], msend.at[f], mrecv.at[f], after)
+        [
+            remote(
+                mb.at[2 + f, pl.ds(COLS + i * TILE, TILE)],
+                mb.at[f, pl.ds(COLS + i * TILE, TILE)],
+                msend.at[2 * f + i],
+                mrecv.at[2 * f + i],
+                after,
+            )
+            for i in range(2)
+        ]
         for f in range(2)
     ]
-
     for n in range(2):
         forwards[2 * n].wait_recv()
 
     for f in (1, 0):
         q = query[half[f], :]
         tilt = dot_t(q, side_wide)
-        bias = [tilt[:, 0:1], tilt[:, 128:129]]
-        scores, values = [], []
-
+        keys, values = [], []
         for n in range(2):
-            cam_copies[f][n].wait_recv()
+            for i in (0, 1) if f == 1 else (2,):
+                cam_copies[i][n].wait_recv()
             tag = nbr[n, f, pl.ds(CELLS, 48), :].astype(F32)
             scale_there = fw_in[n, 1:2, :]
             factor = tag[32:33] * scale_there
             offset = ((tag[0:1] + tag[16:17]) - fw_in[n, 0:1, :]) * scale_there + shift[...]
             rows = silu(jnp.log(nbr[n, f, pl.ds(0, CELLS), :].astype(F32)) * factor + offset)
-            keys = dot(rows, wk[...]).astype(BF16)
+            keys.append(dot(rows, wk[...]).astype(BF16))
             values.append(dot(rows, wv[...]).astype(BF16))
-            scores.append((dot_t(q, keys) + bias[n]) * CHANS ** (-0.5))
-        top = jnp.maximum(
-            jnp.max(scores[0], axis=1, keepdims=True), jnp.max(scores[1], axis=1, keepdims=True)
-        )
-        expo = [jnp.exp(s - top) for s in scores]
-        total = jnp.sum(expo[0], axis=1, keepdims=True) + jnp.sum(expo[1], axis=1, keepdims=True)
-        inverse = 1.0 / total
-        attended = (
-            dot((expo[0] * inverse).astype(BF16), values[0])
-            + dot((expo[1] * inverse).astype(BF16), values[1])
-        ).astype(BF16)
-        mixed = hid[half[f], :].astype(F32) + dot(attended, wo[...])
-        mb[2 + f, inner, :] = mixed.astype(BF16)
-
-        @pl.when(jnp.logical_not(is_last))
-        def _():
-            mixed_halo[f].start()
-
+        for i in range(2):
+            part_rows = slice(i * TILE, (i + 1) * TILE)
+            bias = [tilt[part_rows, 0:1], tilt[part_rows, 128:129]]
+            raw = [dot_t(q[part_rows], keys[n]) for n in range(2)]
+            tops = [jnp.max(raw[n], axis=1, keepdims=True) + bias[n] for n in range(2)]
+            top = jnp.maximum(tops[0], tops[1])
+            expo = [jnp.exp2(raw[n] * SCORE - (top - bias[n]) * SCORE) for n in range(2)]
+            total = jnp.sum(expo[0], axis=1, keepdims=True) + jnp.sum(
+                expo[1], axis=1, keepdims=True
+            )
+            inverse = 1.0 / total
+            attended = (
+                dot((expo[0] * inverse).astype(BF16), values[0])
+                + dot((expo[1] * inverse).astype(BF16), values[1])
+            ).astype(BF16)
+            rows = pl.ds(f * CELLS + i * TILE, TILE)
+            mixed = hid[rows, :].astype(F32) + dot(attended, wo[...])
+            mb[2 + f, pl.ds(COLS + i * TILE, TILE), :] = mixed.astype(BF16)
+
+            @pl.when(jnp.logical_not(is_last))
+            def _():
+                mixed_halo[f][i].start()
+
+    loads[14].wait()
     part[half[0], :] = conv_terms(mb, w2, [(2, 2)])
     part[half[1], :] = conv_terms(mb, w2, [(3, 2), (2, 1)])
 
@@ -406,7 +438,8 @@
 
     @pl.when(jnp.logical_not(is_first))
     def _():
-        mixed_halo[1].wait_recv()
+        for copy in mixed_halo[1]:
+            copy.wait_recv()
 
     total = part[half[1], :] + conv_terms(mb, w2, [(1, 0)])
     out_ref[half[1], :] = (xb[3, inner, :].astype(F32) + total).astype(BF16)
@@ -414,13 +447,14 @@
 
     @pl.when(jnp.logical_not(is_first))
     def _():
-        mixed_halo[0].wait_recv()
+        for copy in mixed_halo[0]:
+            copy.wait_recv()
 
     total = part[half[0], :] + conv_terms(mb, w2, [(0, 0)])
     out_ref[half[0], :] = (xb[2, inner, :].astype(F32) + total).astype(BF16)
 
-    for f in range(2):
-        for copy in cam_copies[f]:
+    for i in range(3):
+        for copy in cam_copies[i]:
             copy.wait_send()
 
     @pl.when(core == 0)
@@ -438,7 +472,8 @@
     def _():
         for f in range(2):
             halo[f].wait_send()
-            mixed_halo[f].wait_send()
+            for copy in mixed_halo[f]:
+                copy.wait_send()
 
 
 def on_device(
@@ -496,12 +531,12 @@
             dma((2,)),
             dma((tms,)),
             dma((tms // 2,)),
+            dma((6,)),
+            dma((6,)),
+            dma((4,)),
+            dma((2,)),
             dma((4,)),
             dma((4,)),
-            dma((4,)),
-            dma((2,)),
-            dma((2,)),
-            dma((2,)),
         ],
         compiler_params=pltpu.CompilerParams(
             collective_id=0, has_side_effects=True, vmem_limit_bytes=62 * 2**20

time: 46.3 us -> 45 us (0.972)
  Pallas kernels: 44.3 us -> 43 us
    pallas_call x1, Pallas kernels: 44.3 us -> 43 us  [on_device(): pl.pallas_call(functools.partial(block_kernel, cams, tms), out_shape=jax....]
where the time goes in v4:
time: 45 us; the launch traced here: 44.9 us
  Pallas kernels  43 us (96%)
  local copies, waits for them, and re-layouts  1.87 us (4%)
    pallas_call x1, Pallas kernels, on_device(): pl.pallas_call(functools.partial(block_kernel, cams, tms), out_shape=jax....  43 us
    unnamed x1, local copies, waits for them, and re-layouts  1.87 us

profile of v4, /device:TPU:32, one launch (start us, length us, event | category | flops | bytes accessed | tf_op | source)
XLA Modules:
  0.0 44.9 jit_solution(7547030727940682295)
XLA Ops:
  0.0 43.0 %shard_map.118 = bf16[1024,256]{1,0:T(8,128)(2,1)} custom-call(bf16[1024,256]{1,0:T(8,128)(2,1)} %bitcast.9, s32[8]{0:T(128)} %place_ref.1, bf16[9,768,256]{2,1,0:T(8,128)(2,1)} %bitcast.7, bf16[9,768,256]{2,1,0:T(8,128)(2,1)} %bitcast.8, f32[1,256]{1,0:T(1,128)} %bitcast.10, f32[1,256]{1,0:T(1,128)} %bitcast.11, bf16[256,256]{1,0:T(8,128)(2,1)} %wq_ref.1, ...), custom_call_target="tpu_custom_call" | custom-call | flops 9126805504 | bytes 9437184 | tf_op jit(solution)/shard_map/pallas_call | solution.py:499
  43.0 1.9 %copy.14 = bf16[1,2,16,32,256]{4,3,2,1,0:T(8,128)(2,1)} copy(bf16[1,2,16,32,256]{4,3,2,1,0:T(8,128)(2,1)} %bitcast.6) | data formatting | bytes 1048576

commit v5 on v4

--- a/solution.py
+++ b/solution.py
@@ -154,7 +154,7 @@
         pl.semaphore_signal(barrier, inc=1, device_id=to, device_id_type=MESH)
 
     halo = [
-        remote(lat_ref.at[half[f]], xb.at[f, inner], hsend.at[f], hrecv.at[f], after)
+        remote(xb.at[2 + f, inner], xb.at[f, inner], hsend.at[f], hrecv.at[f], after)
         for f in range(2)
     ]
 
@@ -178,6 +178,9 @@
             greet(later(2 * i + tms - 1))
         pl.semaphore_wait(barrier, 6)
 
+    for copy in loads[:2]:
+        copy.wait()
+
     @pl.when(jnp.logical_not(is_last))
     def _():
         halo[1].start()
@@ -190,8 +193,7 @@
         for at in (0, COLS + CELLS):
             xb[slot, pl.ds(at, COLS), :] = zero
             mb[slot, pl.ds(at, COLS), :] = zero
-    for copy in loads[:3]:
-        copy.wait()
+    loads[2].wait()
     first[half[0], :] = conv_terms(xb, w1, [(2, 2)])
     loads[3].wait()
     first[half[1], :] = conv_terms(xb, w1, [(3, 2), (2, 1)])
@@ -219,19 +221,20 @@
 
     def encode(f):
         rows = first[half[f], :]
-        code[f, pl.ds(CELLS, 16), :] = jnp.broadcast_to(means[f], (16, CHANS)).astype(BF16)
-        high = code[f, pl.ds(CELLS, 16), :].astype(F32)[0:1]
-        code[f, pl.ds(CELLS + 16, 16), :] = jnp.broadcast_to(means[f] - high, (16, CHANS)).astype(
-            BF16
-        )
-        rows = rows - (high + code[f, pl.ds(CELLS + 16, 16), :].astype(F32)[0:1])
+        marks = pl.ds(CELLS, 16)
+        code[f, marks, :] = jnp.broadcast_to(means[f], (16, CHANS)).astype(BF16)
+        low = means[f] - code[f, marks, :].astype(F32)[0:1]
+        line = lax.broadcasted_iota(jnp.int32, (16, CHANS), 0)
+        code[f, marks, :] = jnp.where(line < 8, means[f], low).astype(BF16)
+        tag = code[f, marks, :].astype(F32)
+        rows = rows - (tag[0:1] + tag[8:9])
         reach = jnp.max(jnp.abs(rows), axis=0, keepdims=True)
         step = jnp.maximum(reach * (1.01 / SPAN), 1e-30)
-        code[f, pl.ds(CELLS + 32, 16), :] = jnp.broadcast_to(step, (16, CHANS)).astype(BF16)
-        step = code[f, pl.ds(CELLS + 32, 16), :].astype(F32)[0:1]
+        code[f, marks, :] = jnp.where(line < 12, tag, step).astype(BF16)
+        step = code[f, marks, :].astype(F32)[12:13]
         code[f, pl.ds(0, CELLS), :] = jnp.exp(rows * (1.0 / step)).astype(BF16)
 
-    pieces = [(1, pl.ds(0, CUT)), (1, pl.ds(CUT, CELLS + 48 - CUT)), (0, pl.ds(0, CELLS + 48))]
+    pieces = [(1, pl.ds(0, CUT)), (1, pl.ds(CUT, CELLS + 16 - CUT)), (0, pl.ds(0, CELLS + 16))]
     cam_copies = [
         [
             remote(
@@ -387,20 +390,21 @@
         ]
         for f in range(2)
     ]
+    tilts = [dot_t(query[half[f], :], side_wide) for f in range(2)]
     for n in range(2):
         forwards[2 * n].wait_recv()
 
     for f in (1, 0):
         q = query[half[f], :]
-        tilt = dot_t(q, side_wide)
+        tilt = tilts[f]
         keys, values = [], []
         for n in range(2):
             for i in (0, 1) if f == 1 else (2,):
                 cam_copies[i][n].wait_recv()
-            tag = nbr[n, f, pl.ds(CELLS, 48), :].astype(F32)
+            tag = nbr[n, f, pl.ds(CELLS, 16), :].astype(F32)
             scale_there = fw_in[n, 1:2, :]
-            factor = tag[32:33] * scale_there
-            offset = ((tag[0:1] + tag[16:17]) - fw_in[n, 0:1, :]) * scale_there + shift[...]
+            factor = tag[12:13] * scale_there
+            offset = ((tag[0:1] + tag[8:9]) - fw_in[n, 0:1, :]) * scale_there + shift[...]
             rows = silu(jnp.log(nbr[n, f, pl.ds(0, CELLS), :].astype(F32)) * factor + offset)
             keys.append(dot(rows, wk[...]).astype(BF16))
             values.append(dot(rows, wv[...]).astype(BF16))
@@ -508,8 +512,8 @@
             pltpu.VMEM((9, 3 * CHANS, CHANS), BF16),
             pltpu.VMEM((2 * CELLS, CHANS), F32),
             pltpu.VMEM((2 * CELLS, CHANS), F32),
-            pltpu.VMEM((2, CELLS + 48, CHANS), BF16),
-            pltpu.VMEM((2, 2, CELLS + 48, CHANS), BF16),
+            pltpu.VMEM((2, CELLS + 16, CHANS), BF16),
+            pltpu.VMEM((2, 2, CELLS + 16, CHANS), BF16),
             pltpu.VMEM((2 * CELLS, CHANS), BF16),
             pltpu.VMEM((2 * CELLS, CHANS), BF16),
             pltpu.VMEM((2, CHANS), F32),

time: 45 us -> 44.4 us (0.987)
  Pallas kernels: 43 us -> 42.4 us
    pallas_call x1, Pallas kernels: 43 us -> 42.4 us  [on_device(): pl.pallas_call(functools.partial(block_kernel, cams, tms), out_shape=jax....]
where the time goes in v5:
time: 44.4 us; the launch traced here: 44.3 us
  Pallas kernels  42.4 us (95%)
  local copies, waits for them, and re-layouts  1.87 us (4%)
    pallas_call x1, Pallas kernels, on_device(): pl.pallas_call(functools.partial(block_kernel, cams, tms), out_shape=jax....  42.4 us
    unnamed x1, local copies, waits for them, and re-layouts  1.87 us

profile of v5, /device:TPU:32, one launch (start us, length us, event | category | flops | bytes accessed | tf_op | source)
XLA Modules:
  0.0 44.3 jit_solution(7754560364040417527)
XLA Ops:
  0.0 42.4 %shard_map.118 = bf16[1024,256]{1,0:T(8,128)(2,1)} custom-call(bf16[1024,256]{1,0:T(8,128)(2,1)} %bitcast.9, s32[8]{0:T(128)} %place_ref.1, bf16[9,768,256]{2,1,0:T(8,128)(2,1)} %bitcast.7, bf16[9,768,256]{2,1,0:T(8,128)(2,1)} %bitcast.8, f32[1,256]{1,0:T(1,128)} %bitcast.10, f32[1,256]{1,0:T(1,128)} %bitcast.11, bf16[256,256]{1,0:T(8,128)(2,1)} %wq_ref.1, ...), custom_call_target="tpu_custom_call" | custom-call | flops 9126805504 | bytes 9437184 | tf_op jit(solution)/shard_map/pallas_call | solution.py:503
  42.4 1.9 %copy.14 = bf16[1,2,16,32,256]{4,3,2,1,0:T(8,128)(2,1)} copy(bf16[1,2,16,32,256]{4,3,2,1,0:T(8,128)(2,1)} %bitcast.6) | data formatting | bytes 1048576

commit v6 on v5

--- a/solution.py
+++ b/solution.py
@@ -286,9 +286,10 @@
         st[0, 0:1, :] = mean_chip
         st[0, 1:2, :] = square_chip
         for i in far_first:
-            swaps[i].start()
             swaps[i + chips - 1].start()
         swaps[0].start()
+        for i in far_first:
+            swaps[i].start()
 
     @pl.when(core == 1)
     def _():
@@ -397,7 +398,7 @@
     for f in (1, 0):
         q = query[half[f], :]
         tilt = tilts[f]
-        keys, values = [], []
+        there = []
         for n in range(2):
             for i in (0, 1) if f == 1 else (2,):
                 cam_copies[i][n].wait_recv()
@@ -405,9 +406,10 @@
             scale_there = fw_in[n, 1:2, :]
             factor = tag[12:13] * scale_there
             offset = ((tag[0:1] + tag[8:9]) - fw_in[n, 0:1, :]) * scale_there + shift[...]
-            rows = silu(jnp.log(nbr[n, f, pl.ds(0, CELLS), :].astype(F32)) * factor + offset)
-            keys.append(dot(rows, wk[...]).astype(BF16))
-            values.append(dot(rows, wv[...]).astype(BF16))
+            there.append(silu(jnp.log(nbr[n, f, pl.ds(0, CELLS), :].astype(F32)) * factor + offset))
+        keys = [dot(rows, wk[...]).astype(BF16) for rows in there]
+        values = [dot(rows, wv[...]).astype(BF16) for rows in there]
+        attended = []
         for i in range(2):
             part_rows = slice(i * TILE, (i + 1) * TILE)
             bias = [tilt[part_rows, 0:1], tilt[part_rows, 128:129]]
@@ -419,17 +421,21 @@
                 expo[1], axis=1, keepdims=True
             )
             inverse = 1.0 / total
-            attended = (
-                dot((expo[0] * inverse).astype(BF16), values[0])
-                + dot((expo[1] * inverse).astype(BF16), values[1])
-            ).astype(BF16)
+            attended.append(
+                (
+                    dot((expo[0] * inverse).astype(BF16), values[0])
+                    + dot((expo[1] * inverse).astype(BF16), values[1])
+                ).astype(BF16)
+            )
+        for i in range(2):
             rows = pl.ds(f * CELLS + i * TILE, TILE)
-            mixed = hid[rows, :].astype(F32) + dot(attended, wo[...])
+            mixed = hid[rows, :].astype(F32) + dot(attended[i], wo[...])
             mb[2 + f, pl.ds(COLS + i * TILE, TILE), :] = mixed.astype(BF16)
 
-            @pl.when(jnp.logical_not(is_last))
-            def _():
-                mixed_halo[f][i].start()
+        @pl.when(jnp.logical_not(is_last))
+        def _():
+            for copy in mixed_halo[f]:
+                copy.start()
 
     loads[14].wait()
     part[half[0], :] = conv_terms(mb, w2, [(2, 2)])

time: 44.4 us -> 43.9 us (0.989)
  Pallas kernels: 42.4 us -> 41.9 us
    pallas_call x1, Pallas kernels: 42.4 us -> 41.9 us  [on_device(): pl.pallas_call(functools.partial(block_kernel, cams, tms), out_shape=jax....]
where the time goes in v6:
time: 43.9 us; the launch traced here: 43.7 us
  Pallas kernels  41.9 us (95%)
  local copies, waits for them, and re-layouts  1.87 us (4%)
    pallas_call x1, Pallas kernels, on_device(): pl.pallas_call(functools.partial(block_kernel, cams, tms), out_shape=jax....  41.9 us
    unnamed x1, local copies, waits for them, and re-layouts  1.87 us

profile of v6, /device:TPU:32, one launch (start us, length us, event | category | flops | bytes accessed | tf_op | source)
XLA Modules:
  0.0 43.7 jit_solution(7129286261648905148)
XLA Ops:
  0.0 41.9 %shard_map.118 = bf16[1024,256]{1,0:T(8,128)(2,1)} custom-call(bf16[1024,256]{1,0:T(8,128)(2,1)} %bitcast.9, s32[8]{0:T(128)} %place_ref.1, bf16[9,768,256]{2,1,0:T(8,128)(2,1)} %bitcast.7, bf16[9,768,256]{2,1,0:T(8,128)(2,1)} %bitcast.8, f32[1,256]{1,0:T(1,128)} %bitcast.10, f32[1,256]{1,0:T(1,128)} %bitcast.11, bf16[256,256]{1,0:T(8,128)(2,1)} %wq_ref.1, ...), custom_call_target="tpu_custom_call" | custom-call | flops 9126805504 | bytes 9437184 | tf_op jit(solution)/shard_map/pallas_call | solution.py:509
  41.9 1.9 %copy.14 = bf16[1,2,16,32,256]{4,3,2,1,0:T(8,128)(2,1)} copy(bf16[1,2,16,32,256]{4,3,2,1,0:T(8,128)(2,1)} %bitcast.6) | data formatting | bytes 1048576

commit v7 on v6

--- a/solution.py
+++ b/solution.py
@@ -17,6 +17,7 @@
 SPAN = 85.0
 CUT = 256
 TILE = 256
+CHUNKS = ((0, TILE + COLS), (TILE + COLS, CELLS - TILE - COLS))
 SCORE = 1.4426950408889634 / 16.0
 
 
@@ -28,20 +29,20 @@
     return lax.dot_general(a, b, (((1,), (1,)), ((), ())), preferred_element_type=F32)
 
 
-def conv_terms(buf, w, terms):
+def conv_terms(buf, w, terms, at=0, size=CELLS):
     parts = []
     for ds in range(3):
-        acc = jnp.zeros((CELLS, CHANS), F32)
+        acc = jnp.zeros((size, CHANS), F32)
         for slot, dt in terms:
             for dr in range(3):
                 acc += dot(
-                    buf[slot, pl.ds(dr * COLS, CELLS), :],
+                    buf[slot, pl.ds(at + dr * COLS, size), :],
                     w[dt * 3 + dr, pl.ds(ds * CHANS, CHANS), :],
                 )
         parts.append(acc)
-    col = lax.rem(lax.broadcasted_iota(jnp.int32, (CELLS, CHANS), 0), COLS)
+    col = lax.rem(lax.broadcasted_iota(jnp.int32, (size, CHANS), 0), COLS)
     left = jnp.where(col == 0, 0.0, pltpu.roll(parts[0], 1, 0))
-    right = jnp.where(col == COLS - 1, 0.0, pltpu.roll(parts[2], CELLS - 1, 0))
+    right = jnp.where(col == COLS - 1, 0.0, pltpu.roll(parts[2], size - 1, 0))
     return parts[1] + left + right
 
 
@@ -154,8 +155,14 @@
         pl.semaphore_signal(barrier, inc=1, device_id=to, device_id_type=MESH)
 
     halo = [
-        remote(xb.at[2 + f, inner], xb.at[f, inner], hsend.at[f], hrecv.at[f], after)
-        for f in range(2)
+        remote(
+            xb.at[2 + f, pl.ds(COLS + at, size)],
+            xb.at[f, pl.ds(COLS + at, size)],
+            hsend.at[i],
+            hrecv.at[i],
+            after,
+        )
+        for i, (f, at, size) in enumerate(((1, 0, CELLS),) + tuple((0,) + c for c in CHUNKS))
     ]
 
     @pl.when(core == 0)
@@ -183,8 +190,8 @@
 
     @pl.when(jnp.logical_not(is_last))
     def _():
-        halo[1].start()
-        halo[0].start()
+        for copy in halo:
+            copy.start()
 
     for copy in loads[5:14]:
         copy.start()
@@ -206,7 +213,7 @@
 
     @pl.when(jnp.logical_not(is_first))
     def _():
-        halo[1].wait_recv()
+        halo[0].wait_recv()
 
     first[half[1], :] += conv_terms(xb, w1, [(1, 0)])
     first[half[0], :] += conv_terms(xb, w1, [(1, 1)])
@@ -256,11 +263,13 @@
     measure(1)
 
 
-    @pl.when(jnp.logical_not(is_first))
-    def _():
-        halo[0].wait_recv()
-
-    first[half[0], :] += conv_terms(xb, w1, [(0, 0)])
+    for i in range(2):
+
+        @pl.when(jnp.logical_not(is_first))
+        def _():
+            halo[1 + i].wait_recv()
+
+        first[pl.ds(i * TILE, TILE), :] += conv_terms(xb, w1, [(0, 0)], i * TILE, TILE)
     measure(0)
 
     def joined(mean_a, mean_b, square_a, square_b, count):
@@ -381,13 +390,13 @@
     mixed_halo = [
         [
             remote(
-                mb.at[2 + f, pl.ds(COLS + i * TILE, TILE)],
-                mb.at[f, pl.ds(COLS + i * TILE, TILE)],
+                mb.at[2 + f, pl.ds(COLS + at, size)],
+                mb.at[f, pl.ds(COLS + at, size)],
                 msend.at[2 * f + i],
                 mrecv.at[2 * f + i],
                 after,
             )
-            for i in range(2)
+            for i, (at, size) in enumerate(CHUNKS)
         ]
         for f in range(2)
     ]
@@ -455,13 +464,15 @@
     out_ref[half[1], :] = (xb[3, inner, :].astype(F32) + total).astype(BF16)
     part[half[0], :] += conv_terms(mb, w2, [(1, 1)])
 
-    @pl.when(jnp.logical_not(is_first))
-    def _():
-        for copy in mixed_halo[0]:
-            copy.wait_recv()
-
-    total = part[half[0], :] + conv_terms(mb, w2, [(0, 0)])
-    out_ref[half[0], :] = (xb[2, inner, :].astype(F32) + total).astype(BF16)
+    for i in range(2):
+
+        @pl.when(jnp.logical_not(is_first))
+        def _():
+            mixed_halo[0][i].wait_recv()
+
+        rows = pl.ds(i * TILE, TILE)
+        total = part[rows, :] + conv_terms(mb, w2, [(0, 0)], i * TILE, TILE)
+        out_ref[rows, :] = (xb[2, pl.ds(COLS + i * TILE, TILE), :].astype(F32) + total).astype(BF16)
 
     for i in range(3):
         for copy in cam_copies[i]:
@@ -480,8 +491,9 @@
 
     @pl.when(jnp.logical_not(is_last))
     def _():
+        for copy in halo:
+            copy.wait_send()
         for f in range(2):
-            halo[f].wait_send()
             for copy in mixed_halo[f]:
                 copy.wait_send()
 
@@ -536,8 +548,8 @@
             pltpu.VMEM((cams, CHANS), F32),
             pltpu.VMEM((2, CHANS), BF16),
             dma((15,)),
-            dma((2,)),
-            dma((2,)),
+            dma((3,)),
+            dma((3,)),
             dma((2,)),
             dma((tms,)),
             dma((tms // 2,)),

time: 43.9 us -> 43.1 us (0.982)
  Pallas kernels: 41.9 us -> 41.1 us
    pallas_call x1, Pallas kernels: 41.9 us -> 41.1 us  [on_device(): pl.pallas_call(functools.partial(block_kernel, cams, tms), out_shape=jax....]
where the time goes in v7:
time: 43.1 us; the launch traced here: 43 us
  Pallas kernels  41.1 us (95%)
  local copies, waits for them, and re-layouts  1.87 us (4%)
    pallas_call x1, Pallas kernels, on_device(): pl.pallas_call(functools.partial(block_kernel, cams, tms), out_shape=jax....  41.1 us
    unnamed x1, local copies, waits for them, and re-layouts  1.87 us

profile of v7, /device:TPU:32, one launch (start us, length us, event | category | flops | bytes accessed | tf_op | source)
XLA Modules:
  0.0 43.0 jit_solution(12711103437621522368)
XLA Ops:
  0.0 41.1 %shard_map.118 = bf16[1024,256]{1,0:T(8,128)(2,1)} custom-call(bf16[1024,256]{1,0:T(8,128)(2,1)} %bitcast.9, s32[8]{0:T(128)} %place_ref.1, bf16[9,768,256]{2,1,0:T(8,128)(2,1)} %bitcast.7, bf16[9,768,256]{2,1,0:T(8,128)(2,1)} %bitcast.8, f32[1,256]{1,0:T(1,128)} %bitcast.10, f32[1,256]{1,0:T(1,128)} %bitcast.11, bf16[256,256]{1,0:T(8,128)(2,1)} %wq_ref.1, ...), custom_call_target="tpu_custom_call" | custom-call | flops 9126805504 | bytes 9437184 | tf_op jit(solution)/shard_map/pallas_call | solution.py:521
  41.1 1.9 %copy.14 = bf16[1,2,16,32,256]{4,3,2,1,0:T(8,128)(2,1)} copy(bf16[1,2,16,32,256]{4,3,2,1,0:T(8,128)(2,1)} %bitcast.6) | data formatting | bytes 1048576

commit v8 on v7

--- a/solution.py
+++ b/solution.py
@@ -263,19 +263,24 @@
     measure(1)
 
 
+    tile_means, tile_squares = [], []
     for i in range(2):
 
         @pl.when(jnp.logical_not(is_first))
         def _():
             halo[1 + i].wait_recv()
 
-        first[pl.ds(i * TILE, TILE), :] += conv_terms(xb, w1, [(0, 0)], i * TILE, TILE)
-    measure(0)
+        rows = pl.ds(i * TILE, TILE)
+        first[rows, :] += conv_terms(xb, w1, [(0, 0)], i * TILE, TILE)
+        tile_means.append(jnp.sum(first[rows, :], axis=0, keepdims=True) / TILE)
+        dev = first[rows, :] - tile_means[i]
+        tile_squares.append(jnp.sum(dev * dev, axis=0, keepdims=True))
 
     def joined(mean_a, mean_b, square_a, square_b, count):
         gap = mean_b - mean_a
         return 0.5 * (mean_a + mean_b), square_a + square_b + (0.5 * count) * (gap * gap)
 
+    means[0], squares[0] = joined(*tile_means, *tile_squares, TILE)
     mean_here, square_here = joined(means[0], means[1], squares[0], squares[1], CELLS)
     hand = remote(own, mate, psem.at[0], psem.at[1], (cam, pair))
     own[0:1, :] = mean_here

time: 43.1 us -> 43 us (level)
  no operation moved by 1% of the time
where the time goes in v8:
time: 43 us; the launch traced here: 42.9 us
  Pallas kernels  41 us (95%)
  local copies, waits for them, and re-layouts  1.87 us (4%)
    pallas_call x1, Pallas kernels, on_device(): pl.pallas_call(functools.partial(block_kernel, cams, tms), out_shape=jax....  41 us
    unnamed x1, local copies, waits for them, and re-layouts  1.87 us

profile of v8, /device:TPU:32, one launch (start us, length us, event | category | flops | bytes accessed | tf_op | source)
XLA Modules:
  0.0 42.9 jit_solution(12744901119512378116)
XLA Ops:
  0.0 41.0 %shard_map.118 = bf16[1024,256]{1,0:T(8,128)(2,1)} custom-call(bf16[1024,256]{1,0:T(8,128)(2,1)} %bitcast.9, s32[8]{0:T(128)} %place_ref.1, bf16[9,768,256]{2,1,0:T(8,128)(2,1)} %bitcast.7, bf16[9,768,256]{2,1,0:T(8,128)(2,1)} %bitcast.8, f32[1,256]{1,0:T(1,128)} %bitcast.10, f32[1,256]{1,0:T(1,128)} %bitcast.11, bf16[256,256]{1,0:T(8,128)(2,1)} %wq_ref.1, ...), custom_call_target="tpu_custom_call" | custom-call | flops 9126805504 | bytes 9437184 | tf_op jit(solution)/shard_map/pallas_call | solution.py:526
  41.0 1.9 %copy.14 = bf16[1,2,16,32,256]{4,3,2,1,0:T(8,128)(2,1)} copy(bf16[1,2,16,32,256]{4,3,2,1,0:T(8,128)(2,1)} %bitcast.6) | data formatting | bytes 1048576
